TPU v7x, 256 devices: a whole 4x4x8 slice. The times are simulated.
256 devices in a mesh: mesh: 64 (over z, y, core), samp: 4 (over x).
Axes of the slice: x: 4, y: 4, z: 8, core: 2. Of those that a mesh axis runs over, the one named last changes fastest.
Arguments:
- traces: bfloat16 [320, 128, 8192], P('mesh', None, 'samp'), may hold values from -6 to 6
- sketch: bfloat16 [8192, 256], P('samp'), may hold values from -0.0625 to 0.0625
- face_port: int32 [320], P('mesh'), may hold values from 0 to 63, as said below
- face_pos: int32 [320], P('mesh'), may hold values from 0 to 3
- tile_count: int32 [64], P('mesh'), may hold values from 0 to 5, as said below
- port_owner: int32 [64], replicated, may hold values from 0 to 63, as said below
Outputs:
- port_bases: float32 [128, 512, 256], P('mesh')
Inputs may be any that keep to these rules, and one draw needn't show every extreme that they name: Ports are numbered like slabs. The used tiles of port p lie on 4 of the 5 slabs p, p + 1, ..., p + 4 (mod 64), one tile on each, positions 0 to 3 rising with the slab. Used slots of a slab come first, in order of rising port distance; unused slots hold 0 in face_port and face_pos. `tile_count`: some slab uses all its slots. `port_owner`: the owner of port p is slab p + 1 or p + 2 (mod 64). No device owns more than 2 ports, and some device owns exactly 2; some slab sends exactly 2 used tiles to one owner.
All inputs are finite; a program needn't handle non-finite values.
Results may differ from a plain program's by a relative error of at most 0.0038.
Values may be sent and summed in bfloat16 or wider, within the bound.
No kernel may reach another device: no remote copies, remote signals or barrier semaphores. Data moves between devices by JAX's collectives and lax.ppermute only.
A program may use at most 64 MiB of HBM per device.

v0:
```python
import jax
import jax.numpy as jnp
from jax import lax
from jax.sharding import PartitionSpec as P

FACES = 4
PORT_MOST = 2


def passed_along(block, axis, distance):
    devices = range(lax.axis_size(axis))
    route = [((i - distance) % len(devices), i) for i in devices]
    return lax.ppermute(block, axis, route)


def orthonormal(port_block, vacant):
    gram_matrix = jnp.dot(port_block.T, port_block, preferred_element_type=jnp.float32)
    rank_width = gram_matrix.shape[0]
    diagonal_shift = 0.1 * jnp.trace(gram_matrix) / rank_width + 1e-06 + vacant.astype(jnp.float32)
    factor = jnp.linalg.cholesky(
        gram_matrix + diagonal_shift * jnp.eye(rank_width, dtype=jnp.float32)
    )
    return lax.linalg.triangular_solve(
        factor, port_block.astype(jnp.float32), left_side=False, lower=True, transpose_a=True
    )


def route_whole(buffers, positions):
    arrived = []
    for offset_step in range(buffers.shape[0]):
        arrived.append(
            passed_along(
                (buffers[offset_step], positions[offset_step]), "mesh", offset_step + 1 - FACES
            )
        )
    return (jnp.stack([pair[0] for pair in arrived]), jnp.stack([pair[1] for pair in arrived]))


def body(traces, sketch, face_port, face_pos, tile_count, port_owner):
    slot_count = traces.shape[0]
    face_rows = traces.shape[1]
    partial_sum = jnp.einsum("sfk,kr->sfr", traces, sketch, preferred_element_type=jnp.float32)
    port_total = port_owner.shape[0]
    port_ids = jnp.arange(port_total, dtype=jnp.int32)
    same_owner = port_owner[None, :] == port_owner[:, None]
    rank_table = jnp.sum(
        (same_owner & (port_ids[None, :] < port_ids[:, None])).astype(jnp.int32), axis=1
    )
    port_hit = face_port[:, None] == port_ids[None, :]
    owner_of = jnp.sum(jnp.where(port_hit, port_owner[None, :], 0), axis=1)
    rank_of = jnp.sum(jnp.where(port_hit, rank_table[None, :], 0), axis=1)
    filled = jnp.arange(slot_count, dtype=jnp.int32) < tile_count[0]
    peers = lax.axis_size("mesh")
    my_index = lax.axis_index("mesh")
    spans = FACES + 2
    lowest = 1 - FACES
    distance = (owner_of - my_index - lowest) % peers
    targets = distance * PORT_MOST + rank_of
    selector = (
        (targets[None, :] == jnp.arange(spans * PORT_MOST, dtype=jnp.int32)[:, None])
        & filled[None, :]
    ).astype(jnp.bfloat16)
    send_position = jnp.dot(
        selector, (face_pos + 1).astype(jnp.bfloat16), preferred_element_type=jnp.float32
    ).astype(jnp.bfloat16)
    send_position = send_position.reshape(spans, PORT_MOST)
    owned = jnp.sum((port_owner == my_index).astype(jnp.int32))
    vacant = jnp.arange(PORT_MOST, dtype=jnp.int32) >= owned
    summed = lax.psum(partial_sum, "samp").astype(jnp.bfloat16)
    columns = summed.shape[2]
    placed = jnp.einsum("ts,sfr->tfr", selector, summed, preferred_element_type=jnp.float32).astype(
        jnp.bfloat16
    )
    incoming, position = route_whole(
        placed.reshape(spans, PORT_MOST, face_rows, columns), send_position
    )
    assemble_position = position
    columns = incoming.shape[3]
    assemble_position = assemble_position.T.astype(jnp.float32)
    wanted = (jnp.arange(FACES, dtype=jnp.int32) + 1).astype(jnp.float32)
    chooser = (assemble_position[:, None, :] == wanted[None, :, None]).astype(jnp.bfloat16)
    placed = jnp.einsum("kjs,skfr->kjfr", chooser, incoming, preferred_element_type=jnp.float32)
    port_blocks = placed.astype(jnp.bfloat16).reshape(PORT_MOST, FACES * face_rows, columns)
    return jax.vmap(orthonormal)(port_blocks, vacant)


def solution(mesh):
    placed = (P("mesh", None, "samp"), P("samp", None), P("mesh"), P("mesh"), P("mesh"), P())
    return jax.shard_map(
        body, mesh=mesh, in_specs=placed, out_specs=P("mesh", None, None), check_vma=False
    )
```

profile of v0, /device:TPU:1, one launch (start us, length us, event | category | flops | bytes accessed | tf_op | source)
XLA Modules:
  0.0 223.6 jit_solution(8163208146876530409)
XLA Ops:
  1.8 2.9 %fusion.1 = f32[5,128,256]{2,1,0:T(8,128)} fusion(bf16[5,128,2048]{2,1,0:T(8,128)(2,1)S(1)} %copy-done, bf16[2048,256]{1,0:T(8,128)(2,1)} %param.7), kind=kOutput, calls=%fused_computation.9 | convolution fusion | flops 671088640 | bytes 4325376 | tf_op jit(solution)/shard_map/sfk,kr->sfr/dot_general | solution.py:42
  4.7 21.0 %all-reduce.2 = bf16[5,128,256]{2,1,0:T(8,128)(2,1)S(1)} all-reduce(f32[5,128,256]{2,1,0:T(8,128)} %fusion.1), channel_id=1, replica_groups=mesh['mesh'=64,'samp'=4] {'samp'}, use_global_device_ids=true, to_apply=%region_3.4 | all-reduce | flops 163840 | bytes 983040 | tf_op jit(solution)/shard_map/psum | solution.py:69
  27.8 12.7 %collective-permute-start.6 = (bf16[2,128,256]{2,0,1:T(2,128)(2,1)}, bf16[2,128,256]{2,0,1:T(2,128)(2,1)}, u32[]{:S(2)}, u32[]{:S(2)}) collective-permute-start(bf16[2,128,256]{2,0,1:T(2,128)(2,1)} %get-tuple-element.32), channel_id=1, source_target_pairs={{12,0},{16,4},{20,8},{24,12},{28,16},{32,20},{36,24},{40,28},{44,3... | collective-permute-start | bytes 393224 | tf_op jit(solution)/shard_map/ppermute | solution.py:13
  46.9 3.0 %collective-permute-start.1 = (bf16[2]{0:T(256)(128)(2,1)}, bf16[2]{0:T(256)(128)(2,1)}, u32[]{:S(2)}, u32[]{:S(2)}) collective-permute-start(bf16[2]{0:T(256)(128)(2,1)} %get-tuple-element.38), channel_id=1, source_target_pairs={{8,0},{12,4},{16,8},{20,12},{24,16},{28,20},{32,24},{36,28},{40,32... | collective-permute-start | bytes 20 | tf_op jit(solution)/shard_map/ppermute | solution.py:13
  49.9 1.3 copy.46
  51.2 2.8 %collective-permute-start.2 = (bf16[2]{0:T(256)(128)(2,1)}, bf16[2]{0:T(256)(128)(2,1)}, u32[]{:S(2)}, u32[]{:S(2)}) collective-permute-start(bf16[2]{0:T(256)(128)(2,1)} %get-tuple-element.37), channel_id=1, source_target_pairs={{4,0},{8,4},{12,8},{16,12},{20,16},{24,20},{28,24},{32,28},{36,32}... | collective-permute-start | bytes 20 | tf_op jit(solution)/shard_map/ppermute | solution.py:13
  56.5 1.3 copy.48
  57.7 1.2 copy.49
  59.0 2.0 collective-permute-done.4
  61.0 1.3 copy.50
  62.3 5.1 %collective-permute-done.5 = bf16[2]{0:T(256)(128)(2,1)} collective-permute-done((bf16[2]{0:T(256)(128)(2,1)}, bf16[2]{0:T(256)(128)(2,1)}, u32[]{:S(2)}, u32[]{:S(2)}) %collective-permute-start.5) | collective-permute-done | bytes 36 | tf_op jit(solution)/shard_map/ppermute | solution.py:13
  67.3 2.3 %collective-permute-start.10 = (bf16[2,128,256]{2,0,1:T(2,128)(2,1)S(1)}, bf16[2,128,256]{2,0,1:T(2,128)(2,1)}, u32[]{:S(2)}, u32[]{:S(2)}) collective-permute-start(bf16[2,128,256]{2,0,1:T(2,128)(2,1)S(1)} %get-tuple-element.28), channel_id=1, source_target_pairs={{252,0},{0,4},{4,8},{8,12},{12,16},{16,20},{20,24},{24,28},{28,32}... | collective-permute-start | bytes 393224 | tf_op jit(solution)/shard_map/ppermute | solution.py:13
  69.6 1.3 copy.51
  70.9 1.3 stack.48
  78.0 6.8 %collective-permute-done.11 = bf16[2,128,256]{2,0,1:T(2,128)(2,1)S(1)} collective-permute-done((bf16[2,128,256]{2,0,1:T(2,128)(2,1)S(1)}, bf16[2,128,256]{2,0,1:T(2,128)(2,1)S(1)}, u32[]{:S(2)}, u32[]{:S(2)}) %collective-permute-start.11) | collective-permute-done | bytes 131104 | tf_op jit(solution)/shard_map/ppermute | solution.py:13
  84.9 1.7 convolution_convert_fusion.1
  86.7 1.7 select_reduce_fusion
  88.4 2.0 copy.56
  90.5 1.3 fusion.32
  91.7 1.4 fusion.5
  94.0 23.5 %custom-call.16 = f32[2,128,128]{2,1,0:T(8,128)S(1)} custom-call(f32[2,128,128]{2,1,0:T(8,128)S(1)} %cholesky.119), custom_call_target="Cholesky" | custom-call | tf_op jit(solution)/shard_map/vmap(jit(cholesky))/cholesky | solution.py:20
  118.3 20.3 %custom-call.17 = f32[2,1,128,128]{2,3,1,0:T(8,128)} custom-call(f32[2,1,128,128]{3,2,1,0:T(8,128)S(1)} %select_bitcast_fusion), custom_call_target="InvertDiagBlocksLowerTriangular" | custom-call | tf_op jit(solution)/shard_map/vmap(jit(cholesky))/cholesky | solution.py:20
  138.6 1.9 constant_dynamic-update-slice_fusion.1
  140.5 1.9 convolution_subtract_fusion.1
  142.4 24.3 %custom-call.18 = f32[2,128,128]{2,1,0:T(8,128)S(1)} custom-call(f32[2,128,128]{2,1,0:T(8,128)} %convolution_subtract_fusion.1), custom_call_target="Cholesky" | custom-call | tf_op jit(solution)/shard_map/vmap(jit(cholesky))/cholesky | solution.py:20
  167.6 2.0 select_select_fusion
  169.7 7.3 %while.1 = (s32[]{:T(128)}, f32[2,256,256]{2,1,0:T(8,128)}, s32[2,2]{1,0:T(2,128)S(1)}, f32[2,2,128,128]{3,2,0,1:T(8,128)}, s32[]{:T(128)}) while((s32[]{:T(128)}, f32[2,256,256]{2,1,0:T(8,128)}, s32[2,2]{1,0:T(2,128)S(1)}, f32[2,2,128,128]{3,2,0,1:T(8,128)}, s32[]{:T(128)}) %tuple.35), condition=%wide.while_cond, body=%wide.while_body.sunk | while | flops 2 | bytes 263777 | solution.py:23
  170.3 3.0 %bitcast_dynamic-update-slice_fusion.8 = f32[2,2,128,128]{3,2,0,1:T(8,128)} fusion(f32[2,2,128,128]{3,2,0,1:T(8,128)} %get-tuple-element.83, s32[]{:T(128)} %get-tuple-element.80, f32[2,256,256]{2,1,0:T(8,128)} %get-tuple-element.86, s32[]{:T(128)} %bitcast.79, s32[]{:T(128)} %bitcast.80), kind=kLoop, calls=%fused_computation.clone.1 | loop fusion | bytes 263680 | tf_op jit(solution)/shard_map/vmap()/triangular_solve
  174.0 2.9 %bitcast_dynamic-update-slice_fusion.8 = f32[2,2,128,128]{3,2,0,1:T(8,128)} fusion(f32[2,2,128,128]{3,2,0,1:T(8,128)} %get-tuple-element.83, s32[]{:T(128)} %get-tuple-element.80, f32[2,256,256]{2,1,0:T(8,128)} %get-tuple-element.86, s32[]{:T(128)} %bitcast.79, s32[]{:T(128)} %bitcast.80), kind=kLoop, calls=%fused_computation.clone.1 | loop fusion | bytes 263680 | tf_op jit(solution)/shard_map/vmap()/triangular_solve
  176.9 40.1 %custom-call.19 = f32[2,2,128,128]{2,3,1,0:T(8,128)S(1)} custom-call(f32[2,2,128,128]{3,2,1,0:T(8,128)} %bitcast.85), custom_call_target="InvertDiagBlocksLowerTriangular" | custom-call | tf_op jit(solution)/shard_map/vmap()/triangular_solve | solution.py:23
  217.5 1.9 convolution_subtract_fusion
  221.1 2.5 %copy.63 = f32[2,512,256]{2,1,0:T(8,128)} copy(f32[2,512,256]{1,2,0:T(8,128)} %pad_maximum_fusion) | data formatting | bytes 2097152 | tf_op jit(solution)/shard_map/vmap()/triangular_solve | solution.py:23
  (72 shorter events, 24.0 us)
Async XLA Ops:
  0.0 1.8 copy-start
  1.8 23.9 %copy-start.3 = (s32[5]{0:T(128)S(1)}, s32[5]{0:T(128)}, u32[]{:S(2)}) copy-start(s32[5]{0:T(128)} %param.8) | copy-start | bytes 64
  1.8 23.9 %copy-start.4 = (s32[64]{0:T(128)S(1)}, s32[64]{0:T(128)}, u32[]{:S(2)}) copy-start(s32[64]{0:T(128)} %param.11) | copy-start | bytes 772
  4.7 36.9 %copy-start.5 = (s32[5]{0:T(128)S(1)}, s32[5]{0:T(128)}, u32[]{:S(2)}) copy-start(s32[5]{0:T(128)} %param.9) | copy-start | bytes 64
  27.8 45.1 %collective-permute-start.6 = (bf16[2,128,256]{2,0,1:T(2,128)(2,1)}, bf16[2,128,256]{2,0,1:T(2,128)(2,1)}, u32[]{:S(2)}, u32[]{:S(2)}) collective-permute-start(bf16[2,128,256]{2,0,1:T(2,128)(2,1)} %get-tuple-element.32), channel_id=1, source_target_pairs={{12,0},{16,4},{20,8},{24,12},{28,16},{32,20},{36,24},{40,28},{44,3... | collective-permute-start | bytes 393224 | tf_op jit(solution)/shard_map/ppermute | solution.py:13
  40.5 33.4 %collective-permute-start.7 = (bf16[2,128,256]{2,0,1:T(2,128)(2,1)}, bf16[2,128,256]{2,0,1:T(2,128)(2,1)}, u32[]{:S(2)}, u32[]{:S(2)}) collective-permute-start(bf16[2,128,256]{2,0,1:T(2,128)(2,1)} %get-tuple-element.31), channel_id=1, source_target_pairs={{8,0},{12,4},{16,8},{20,12},{24,16},{28,20},{32,24},{36,28},{40,32... | collective-permute-start | bytes 393224 | tf_op jit(solution)/shard_map/ppermute | solution.py:13
  40.9 34.0 %collective-permute-start.8 = (bf16[2,128,256]{2,0,1:T(2,128)(2,1)S(1)}, bf16[2,128,256]{2,0,1:T(2,128)(2,1)}, u32[]{:S(2)}, u32[]{:S(2)}) collective-permute-start(bf16[2,128,256]{2,0,1:T(2,128)(2,1)S(1)} %get-tuple-element.30), channel_id=1, source_target_pairs={{4,0},{8,4},{12,8},{16,12},{20,16},{24,20},{28,24},{32,28},{36,32}... | collective-permute-start | bytes 393224 | tf_op jit(solution)/shard_map/ppermute | solution.py:13
  40.9 35.0 %collective-permute-start.9 = (bf16[2,128,256]{2,0,1:T(2,128)(2,1)S(1)}, bf16[2,128,256]{2,0,1:T(2,128)(2,1)}, u32[]{:S(2)}, u32[]{:S(2)}) collective-permute-start(bf16[2,128,256]{2,0,1:T(2,128)(2,1)S(1)} %get-tuple-element.29), channel_id=1, source_target_pairs={{0,0},{4,4},{8,8},{12,12},{16,16},{20,20},{24,24},{28,28},{32,32},... | collective-permute-start | bytes 393224 | tf_op jit(solution)/shard_map/ppermute | solution.py:13
  42.4 4.5 %collective-permute-start = (bf16[2]{0:T(256)(128)(2,1)}, bf16[2]{0:T(256)(128)(2,1)}, u32[]{:S(2)}, u32[]{:S(2)}) collective-permute-start(bf16[2]{0:T(256)(128)(2,1)} %get-tuple-element.39), channel_id=1, source_target_pairs={{12,0},{16,4},{20,8},{24,12},{28,16},{32,20},{36,24},{40,28},{44,3... | collective-permute-start | bytes 20 | tf_op jit(solution)/shard_map/ppermute | solution.py:13
  46.9 4.3 %collective-permute-start.1 = (bf16[2]{0:T(256)(128)(2,1)}, bf16[2]{0:T(256)(128)(2,1)}, u32[]{:S(2)}, u32[]{:S(2)}) collective-permute-start(bf16[2]{0:T(256)(128)(2,1)} %get-tuple-element.38), channel_id=1, source_target_pairs={{8,0},{12,4},{16,8},{20,12},{24,16},{28,20},{32,24},{36,28},{40,32... | collective-permute-start | bytes 20 | tf_op jit(solution)/shard_map/ppermute | solution.py:13
  51.2 4.1 %collective-permute-start.2 = (bf16[2]{0:T(256)(128)(2,1)}, bf16[2]{0:T(256)(128)(2,1)}, u32[]{:S(2)}, u32[]{:S(2)}) collective-permute-start(bf16[2]{0:T(256)(128)(2,1)} %get-tuple-element.37), channel_id=1, source_target_pairs={{4,0},{8,4},{12,8},{16,12},{20,16},{24,20},{28,24},{32,28},{36,32}... | collective-permute-start | bytes 20 | tf_op jit(solution)/shard_map/ppermute | solution.py:13
  55.3 2.4 %collective-permute-start.3 = (bf16[2]{0:T(256)(128)(2,1)}, bf16[2]{0:T(256)(128)(2,1)}, u32[]{:S(2)}, u32[]{:S(2)}) collective-permute-start(bf16[2]{0:T(256)(128)(2,1)} %get-tuple-element.36), channel_id=1, source_target_pairs={{0,0},{4,4},{8,8},{12,12},{16,16},{20,20},{24,24},{28,28},{32,32},... | collective-permute-start | bytes 20 | tf_op jit(solution)/shard_map/ppermute | solution.py:13
  57.7 3.2 %collective-permute-start.4 = (bf16[2]{0:T(256)(128)(2,1)}, bf16[2]{0:T(256)(128)(2,1)}, u32[]{:S(2)}, u32[]{:S(2)}) collective-permute-start(bf16[2]{0:T(256)(128)(2,1)} %get-tuple-element.35), channel_id=1, source_target_pairs={{252,0},{0,4},{4,8},{8,12},{12,16},{16,20},{20,24},{24,28},{28,32}... | collective-permute-start | bytes 20 | tf_op jit(solution)/shard_map/ppermute | solution.py:13
  61.0 6.4 %collective-permute-start.5 = (bf16[2]{0:T(256)(128)(2,1)}, bf16[2]{0:T(256)(128)(2,1)}, u32[]{:S(2)}, u32[]{:S(2)}) collective-permute-start(bf16[2]{0:T(256)(128)(2,1)} %get-tuple-element.34), channel_id=1, source_target_pairs={{248,0},{252,4},{0,8},{4,12},{8,16},{12,20},{16,24},{20,28},{24,32... | collective-permute-start | bytes 20 | tf_op jit(solution)/shard_map/ppermute | solution.py:13
  67.3 9.7 %collective-permute-start.10 = (bf16[2,128,256]{2,0,1:T(2,128)(2,1)S(1)}, bf16[2,128,256]{2,0,1:T(2,128)(2,1)}, u32[]{:S(2)}, u32[]{:S(2)}) collective-permute-start(bf16[2,128,256]{2,0,1:T(2,128)(2,1)S(1)} %get-tuple-element.28), channel_id=1, source_target_pairs={{252,0},{0,4},{4,8},{8,12},{12,16},{16,20},{20,24},{24,28},{28,32}... | collective-permute-start | bytes 393224 | tf_op jit(solution)/shard_map/ppermute | solution.py:13
  72.9 11.9 %collective-permute-start.11 = (bf16[2,128,256]{2,0,1:T(2,128)(2,1)S(1)}, bf16[2,128,256]{2,0,1:T(2,128)(2,1)S(1)}, u32[]{:S(2)}, u32[]{:S(2)}) collective-permute-start(bf16[2,128,256]{2,0,1:T(2,128)(2,1)S(1)} %get-tuple-element.27), channel_id=1, source_target_pairs={{248,0},{252,4},{0,8},{4,12},{8,16},{12,20},{16,24},{20,28},{24,32... | collective-permute-start | bytes 393224 | tf_op jit(solution)/shard_map/ppermute | solution.py:13
  88.4 29.8 %copy-start.2 = (pred[128,128]{1,0:T(8,128)(4,1)S(1)}, pred[128,128]{1,0:T(8,128)(4,1)}, u32[]{:S(2)}) copy-start(pred[128,128]{1,0:T(8,128)(4,1)} %iota_compare_fusion.3) | copy-start | bytes 49156
  91.7 77.9 %copy-start.6 = (s32[2]{0:T(128)S(1)}, s32[2]{0:T(128)}, u32[]{:S(2)}) copy-start(s32[2]{0:T(128)} %iota_multiply_fusion) | copy-start | bytes 28
  93.2 0.8 copy-start.1
where the time goes:
time: 224 us
  other arithmetic  120 us (54%)
  local copies, waits for them, and re-layouts  29.7 us (13%)
  starting transfers between devices  23.8 us (11%)
  blocking collectives  21 us (9%)
  waiting for transfers between devices  14.5 us (6%)
  matrix products  13.9 us (6%)
    another operation x10, other arithmetic, orthonormal(): jnp.linalg.cholesky(gram_matrix + diagonal_shift * jnp.eye(rank_width, dt...  69.6 us
    another operation x5, other arithmetic, orthonormal(): lax.linalg.triangular_solve(factor, port_block.astype(jnp.float32), left_...  43.8 us
    ppermute x12, starting transfers between devices, passed_along(): return lax.ppermute(block, axis, route)  23.8 us
    psum x1, blocking collectives, body(): summed = lax.psum(partial_sum, 'samp').astype(jnp.bfloat16)  21 us
    ppermute x12, waiting for transfers between devices, passed_along(): return lax.ppermute(block, axis, route)  14.5 us
    another operation x7, local copies, waits for them, and re-layouts, route_whole(): jnp.stack([pair[1] for pair in arrived])  8.94 us
    another operation x6, local copies, waits for them, and re-layouts  7.25 us
    unnamed x19, local copies, waits for them, and re-layouts  5.94 us
  transfers between devices with their start and end apart: 12, of which 4 were waited for; matrix products, arithmetic and copies ran while one was open for 8% of the time, Pallas kernels for 0%

commit v1 on v0

--- a/solution.py
+++ b/solution.py
@@ -1,6 +1,8 @@
 import jax
 import jax.numpy as jnp
 from jax import lax
+from jax.experimental import pallas as pl
+from jax.experimental.pallas import tpu as pltpu
 from jax.sharding import PartitionSpec as P
 
 FACES = 4
@@ -13,16 +15,98 @@
     return lax.ppermute(block, axis, route)
 
 
-def orthonormal(port_block, vacant):
-    gram_matrix = jnp.dot(port_block.T, port_block, preferred_element_type=jnp.float32)
-    rank_width = gram_matrix.shape[0]
-    diagonal_shift = 0.1 * jnp.trace(gram_matrix) / rank_width + 1e-06 + vacant.astype(jnp.float32)
-    factor = jnp.linalg.cholesky(
-        gram_matrix + diagonal_shift * jnp.eye(rank_width, dtype=jnp.float32)
-    )
-    return lax.linalg.triangular_solve(
-        factor, port_block.astype(jnp.float32), left_side=False, lower=True, transpose_a=True
-    )
+B = 64
+HI = lax.Precision.HIGHEST
+f32 = jnp.float32
+
+def mm(a, b, dims=((1,), (0,)), prec=HI):
+    return lax.dot_general(a, b, (dims, ((), ())), precision=prec, preferred_element_type=f32)
+
+def panel(t0):
+    lane = lax.broadcasted_iota(jnp.int32, (B, 128), 1)
+    row = lax.broadcasted_iota(jnp.int32, (B, 128), 0)
+    t1 = ((lane % B) == row).astype(f32)
+    half = jnp.where(lane < B, 0, B)
+    r0 = [t0[8*i:8*i+8] for i in range(B//8)]
+    r1 = [t1[8*i:8*i+8] for i in range(B//8)]
+    h8 = half[:8]
+    row8 = row[:8]
+    done = []
+    for g in range(B//8):
+        n = B//8 - g
+        C = [[jnp.take_along_axis(r0[g+i], h8 + (8*g+j), axis=1, mode="promise_in_bounds") for i in range(n)] for j in range(8)]
+        for j in range(0, 8, 2):
+            cj, ck = C[j], C[j+1]
+            a, b, d = cj[0][j:j+1], cj[0][j+1:j+2], ck[0][j+1:j+2]
+            inv = 1.0 / (a*d - b*b)
+            i00, i01, i11 = d*inv, -b*inv, a*inv
+            m0 = [x*i00 + y*i01 for x, y in zip(cj, ck)]
+            m1 = [x*i01 + y*i11 for x, y in zip(cj, ck)]
+            keep = row8 > j+1
+            m0[0] = jnp.where(keep, m0[0], 0.0)
+            m1[0] = jnp.where(keep, m1[0], 0.0)
+            for k in range(j+2, 8):
+                p, q = C[k][0][j:j+1], C[k][0][j+1:j+2]
+                C[k] = [c - (x*p + y*q) for c, x, y in zip(C[k], m0, m1)]
+            p0, q0 = r0[g][j:j+1], r0[g][j+1:j+2]
+            p1, q1 = r1[g][j:j+1], r1[g][j+1:j+2]
+            done.append((a, b, d, p1, q1))
+            for i in range(n):
+                if i > 0:
+                    r0[g+i] = r0[g+i] - (m0[i]*p0 + m1[i]*q0)
+                elif j < 6:
+                    r0[g+i] = r0[g+i] - (m0[i]*p0 + m1[i]*q0)
+                r1[g+i] = r1[g+i] - (m0[i]*p1 + m1[i]*q1)
+    rows = []
+    for a, b, d, p1, q1 in done:
+        ra = lax.rsqrt(a)
+        l10 = b * (1.0 / a)
+        rd = lax.rsqrt(d - b*l10)
+        rows.append(p1 * ra)
+        rows.append((q1 - l10*p1) * rd)
+    return jnp.concatenate(rows, axis=0)
+
+def kernel(p_ref, o_ref, s_ref):
+    n = 256
+    row = lax.broadcasted_iota(jnp.int32, (n, n), 0)
+    col = lax.broadcasted_iota(jnp.int32, (n, n), 1)
+    eye = (row == col).astype(f32)
+    for p in range(2):
+        x = p_ref[p]
+        g = mm(x, x, ((0,), (0,)), None)
+        tr = jnp.sum(g * eye)
+        s_ref[p] = g + (0.1 * tr / n + 1e-6) * eye
+    for k in range(n // B):
+        lo, hi = k*B, (k+1)*B
+        t = panel(jnp.concatenate([s_ref[0, lo:hi, lo:hi], s_ref[1, lo:hi, lo:hi]], axis=1))
+        for p in range(2):
+            w = t[:, p*B:(p+1)*B]
+            sk = s_ref[p, lo:hi, :]
+            c = lax.broadcasted_iota(jnp.int32, (B, n), 1)
+            r = lax.broadcasted_iota(jnp.int32, (B, n), 0)
+            sk = jnp.where((c >= lo) & (c < hi), (c - lo == r).astype(f32), sk)
+            y = mm(w, sk)
+            if hi < n:
+                u = mm(s_ref[p, hi:, lo:hi], w, ((1,), (1,)))
+                c2 = lax.broadcasted_iota(jnp.int32, (n-hi, n), 1)
+                old = jnp.where((c2 >= lo) & (c2 < hi), 0.0, s_ref[p, hi:, :])
+                s_ref[p, hi:, :] = old - mm(u, y)
+            s_ref[p, lo:hi, :] = y
+    for p in range(2):
+        w = jnp.where(col <= row, s_ref[p], 0.0)
+        w0 = w.astype(jnp.bfloat16)
+        e = w - w0.astype(f32)
+        w1 = e.astype(jnp.bfloat16)
+        w2 = (e - w1.astype(f32)).astype(jnp.bfloat16)
+        x = p_ref[p]
+        acc = mm(x, w2, ((1,), (1,)), None) + mm(x, w1, ((1,), (1,)), None)
+        o_ref[p] = acc + mm(x, w0, ((1,), (1,)), None)
+
+def solve(p):
+    return pl.pallas_call(kernel, out_shape=jax.ShapeDtypeStruct((2, 512, 256), f32),
+        in_specs=[pl.BlockSpec(memory_space=pltpu.VMEM)], out_specs=pl.BlockSpec(memory_space=pltpu.VMEM),
+        scratch_shapes=[pltpu.VMEM((2, 256, 256), f32)],
+        compiler_params=pltpu.CompilerParams(vmem_limit_bytes=40 << 20))(p)
 
 
 def route_whole(buffers, positions):
@@ -81,7 +165,7 @@
     chooser = (assemble_position[:, None, :] == wanted[None, :, None]).astype(jnp.bfloat16)
     placed = jnp.einsum("kjs,skfr->kjfr", chooser, incoming, preferred_element_type=jnp.float32)
     port_blocks = placed.astype(jnp.bfloat16).reshape(PORT_MOST, FACES * face_rows, columns)
-    return jax.vmap(orthonormal)(port_blocks, vacant)
+    return solve(port_blocks)
 
 
 def solution(mesh):

time: 224 us -> 96.2 us (0.43)
  other arithmetic: 120 us -> 1.82 us
  local copies, waits for them, and re-layouts: 29.7 us -> 12.9 us
  Pallas kernels: 0 us -> 11.5 us
  matrix products: 13.9 us -> 4.77 us
  waiting for transfers between devices: 14.5 us -> 19.1 us
    another operation x15 -> x0, other arithmetic: 113 us -> none  [the longest x10 69.6 us: orthonormal(): jnp.linalg.cholesky(gram_matrix + diagonal_shift * jnp.eye(rank_width, dt...]
    pallas_call x0 -> x1, Pallas kernels: none -> 11.5 us  [solve(): pl.pallas_call(kernel, out_shape=jax.ShapeDtypeStruct((2, 512, 256), f32)...]
    another operation x10 -> x0, local copies, waits for them, and re-layouts: 10.7 us -> none
    another operation x5 -> x0, matrix products: 6.78 us -> none  [the longest x2 3.84 us: orthonormal(): jnp.linalg.cholesky(gram_matrix + diagonal_shift * jnp.eye(rank_width, dt...]
    ppermute x12, waiting for transfers between devices: 14.5 us -> 19.1 us  [passed_along(): return lax.ppermute(block, axis, route)]
    unnamed x19 -> x15, local copies, waits for them, and re-layouts: 5.94 us -> 4.25 us
  transfers between devices with their start and end apart: 12 -> 12, of which waited for: 4 -> 5; matrix products, arithmetic and copies ran while one was open for 8% -> 13% of each run, Pallas kernels for 0% -> 0%
where the time goes in v1:
time: 96.2 us; the launch traced here: 95.8 us
  starting transfers between devices  24.1 us (25%)
  blocking collectives  21 us (22%)
  waiting for transfers between devices  19.1 us (20%)
  local copies, waits for them, and re-layouts  12.9 us (13%)
  Pallas kernels  11.5 us (12%)
  matrix products  4.77 us (5%)
  other arithmetic  1.82 us (2%)
    ppermute x12, starting transfers between devices, passed_along(): return lax.ppermute(block, axis, route)  24.1 us
    psum x1, blocking collectives, body(): summed = lax.psum(partial_sum, 'samp').astype(jnp.bfloat16)  21 us
    ppermute x12, waiting for transfers between devices, passed_along(): return lax.ppermute(block, axis, route)  19.1 us
    pallas_call x1, Pallas kernels, solve(): pl.pallas_call(kernel, out_shape=jax.ShapeDtypeStruct((2, 512, 256), f32)...  11.5 us
    another operation x7, local copies, waits for them, and re-layouts, route_whole(): jnp.stack([pair[1] for pair in arrived])  7.23 us
    unnamed x15, local copies, waits for them, and re-layouts  4.25 us
    dot_general x1, matrix products, body(): jnp.einsum('sfk,kr->sfr', traces, sketch, preferred_element_type=jnp.floa...  2.93 us
  transfers between devices with their start and end apart: 12, of which 5 were waited for; matrix products, arithmetic and copies ran while one was open for 13% of the time, Pallas kernels for 0%

profile of v1, /device:TPU:1, one launch (start us, length us, event | category | flops | bytes accessed | tf_op | source)
XLA Modules:
  0.0 95.8 jit_solution(5044525590298750949)
XLA Ops:
  0.0 1.0 %convert_reduce_fusion = s32[64]{0:T(128)S(1)} fusion(s32[64]{0:T(128)} %param.11), kind=kLoop, calls=%fused_computation.14 | loop fusion | flops 20416 | bytes 512 | tf_op jit(solution)/shard_map/reduce_sum | solution.py:130
  1.8 2.9 %fusion.1 = f32[5,128,256]{2,1,0:T(8,128)} fusion(bf16[5,128,2048]{2,1,0:T(8,128)(2,1)S(1)} %copy-done, bf16[2048,256]{1,0:T(8,128)(2,1)} %param.7), kind=kOutput, calls=%fused_computation.4 | convolution fusion | flops 671088640 | bytes 4325376 | tf_op jit(solution)/shard_map/sfk,kr->sfr/dot_general | solution.py:126
  4.7 21.0 %all-reduce.1 = bf16[5,128,256]{2,1,0:T(8,128)(2,1)S(1)} all-reduce(f32[5,128,256]{2,1,0:T(8,128)} %fusion.1), channel_id=1, replica_groups=mesh['mesh'=64,'samp'=4] {'samp'}, use_global_device_ids=true, to_apply=%region_3.4 | all-reduce | flops 163840 | bytes 983040 | tf_op jit(solution)/shard_map/psum | solution.py:153
  25.9 0.6 convolution_convert_fusion
  26.5 0.5 fusion.24
  27.1 12.8 %collective-permute-start.6 = (bf16[2,128,256]{2,0,1:T(2,128)(2,1)S(1)}, bf16[2,128,256]{2,0,1:T(2,128)(2,1)}, u32[]{:S(2)}, u32[]{:S(2)}) collective-permute-start(bf16[2,128,256]{2,0,1:T(2,128)(2,1)S(1)} %get-tuple-element.12), channel_id=1, source_target_pairs={{12,0},{16,4},{20,8},{24,12},{28,16},{32,20},{36,24},{40,28},{44,3... | collective-permute-start | bytes 393224 | tf_op jit(solution)/shard_map/ppermute | solution.py:15
  39.9 0.5 collective-permute-start.7
  40.6 0.7 fusion.25
  41.2 0.6 collective-permute-start
  41.8 3.9 %collective-permute-done = bf16[2]{0:T(256)(128)(2,1)S(1)} collective-permute-done((bf16[2]{0:T(256)(128)(2,1)S(1)}, bf16[2]{0:T(256)(128)(2,1)S(1)}, u32[]{:S(2)}, u32[]{:S(2)}) %collective-permute-start) | collective-permute-done | bytes 36 | tf_op jit(solution)/shard_map/ppermute | solution.py:15
  45.7 3.0 %collective-permute-start.1 = (bf16[2]{0:T(256)(128)(2,1)}, bf16[2]{0:T(256)(128)(2,1)}, u32[]{:S(2)}, u32[]{:S(2)}) collective-permute-start(bf16[2]{0:T(256)(128)(2,1)} %get-tuple-element.17), channel_id=1, source_target_pairs={{8,0},{12,4},{16,8},{20,12},{24,16},{28,20},{32,24},{36,28},{40,32... | collective-permute-start | bytes 20 | tf_op jit(solution)/shard_map/ppermute | solution.py:15
  48.7 0.7 copy.18
  49.4 0.2 collective-permute-done.1
  49.6 3.3 %collective-permute-start.2 = (bf16[2]{0:T(256)(128)(2,1)}, bf16[2]{0:T(256)(128)(2,1)}, u32[]{:S(2)}, u32[]{:S(2)}) collective-permute-start(bf16[2]{0:T(256)(128)(2,1)} %get-tuple-element.16), channel_id=1, source_target_pairs={{4,0},{8,4},{12,8},{16,12},{20,16},{24,20},{28,24},{32,28},{36,32}... | collective-permute-start | bytes 20 | tf_op jit(solution)/shard_map/ppermute | solution.py:15
  52.9 1.3 %copy.19 = bf16[1,2]{0,1:T(2,128)(2,1)} copy(bf16[1,2]{1,0:T(2,128)(2,1)} %bitcast.4) | data formatting | bytes 8 | tf_op jit(solution)/shard_map/stack | solution.py:120
  54.2 1.2 %collective-permute-start.3 = (bf16[2]{0:T(256)(128)(2,1)}, bf16[2]{0:T(256)(128)(2,1)}, u32[]{:S(2)}, u32[]{:S(2)}) collective-permute-start(bf16[2]{0:T(256)(128)(2,1)} %get-tuple-element.15), channel_id=1, source_target_pairs={{0,0},{4,4},{8,8},{12,12},{16,16},{20,20},{24,24},{28,28},{32,32},... | collective-permute-start | bytes 20 | tf_op jit(solution)/shard_map/ppermute | solution.py:15
  55.4 1.3 %copy.20 = bf16[1,2]{0,1:T(2,128)(2,1)} copy(bf16[1,2]{1,0:T(2,128)(2,1)} %bitcast.5) | data formatting | bytes 8 | tf_op jit(solution)/shard_map/stack | solution.py:120
  56.7 1.2 %copy.21 = bf16[1,2]{0,1:T(2,128)(2,1)} copy(bf16[1,2]{1,0:T(2,128)(2,1)} %bitcast.6) | data formatting | bytes 8 | tf_op jit(solution)/shard_map/stack | solution.py:120
  57.9 1.8 %collective-permute-done.4 = bf16[2]{0:T(256)(128)(2,1)} collective-permute-done((bf16[2]{0:T(256)(128)(2,1)S(1)}, bf16[2]{0:T(256)(128)(2,1)}, u32[]{:S(2)}, u32[]{:S(2)}) %collective-permute-start.4) | collective-permute-done | bytes 36 | tf_op jit(solution)/shard_map/ppermute | solution.py:15
  59.7 0.8 copy.22
  60.4 5.4 %collective-permute-done.5 = bf16[2]{0:T(256)(128)(2,1)} collective-permute-done((bf16[2]{0:T(256)(128)(2,1)S(1)}, bf16[2]{0:T(256)(128)(2,1)}, u32[]{:S(2)}, u32[]{:S(2)}) %collective-permute-start.5) | collective-permute-done | bytes 36 | tf_op jit(solution)/shard_map/ppermute | solution.py:15
  65.9 2.7 %collective-permute-start.10 = (bf16[2,128,256]{2,0,1:T(2,128)(2,1)S(1)}, bf16[2,128,256]{2,0,1:T(2,128)(2,1)}, u32[]{:S(2)}, u32[]{:S(2)}) collective-permute-start(bf16[2,128,256]{2,0,1:T(2,128)(2,1)S(1)} %get-tuple-element.8), channel_id=1, source_target_pairs={{252,0},{0,4},{4,8},{8,12},{12,16},{16,20},{20,24},{24,28},{28,32}... | collective-permute-start | bytes 393224 | tf_op jit(solution)/shard_map/ppermute | solution.py:15
  68.6 0.7 copy.23
  69.3 1.3 %stack.48 = bf16[6,2]{0,1:T(2,128)(2,1)} concatenate(bf16[1,2]{0,1:T(2,128)(2,1)S(1)} %copy.18, bf16[1,2]{0,1:T(2,128)(2,1)} %copy.19, bf16[1,2]{0,1:T(2,128)(2,1)} %copy.20, bf16[1,2]{0,1:T(2,128)(2,1)} %copy.21, bf16[1,2]{0,1:T(2,128)(2,1)S(1)} %copy.22, bf16[1,2]{0,1:T(2,128)(2,1)S(1)} %copy.23), dimensions={0} | concatenate | bytes 48 | tf_op jit(solution)/shard_map/stack | solution.py:120
  70.6 0.6 convert_bitcast_fusion
  71.2 1.0 %bitcast_dynamic-update-slice_fusion.5 = bf16[6,2,128,256]{3,1,2,0:T(2,128)(2,1)S(1)} fusion(bf16[2,128,256]{2,0,1:T(2,128)(2,1)} %collective-permute-done.6), kind=kLoop, calls=%fused_computation.13 | loop fusion | bytes 262144
  72.2 1.0 %bitcast_dynamic-update-slice_fusion.4 = bf16[6,2,128,256]{3,1,2,0:T(2,128)(2,1)S(1)} fusion(bf16[6,2,128,256]{3,1,2,0:T(2,128)(2,1)S(1)} %bitcast_dynamic-update-slice_fusion.5, bf16[2,128,256]{2,0,1:T(2,128)(2,1)} %collective-permute-done.7), kind=kLoop, calls=%fused_computation.12 | loop fusion | bytes 262144
  73.2 1.0 %bitcast_dynamic-update-slice_fusion.3 = bf16[6,2,128,256]{3,1,2,0:T(2,128)(2,1)S(1)} fusion(bf16[6,2,128,256]{3,1,2,0:T(2,128)(2,1)S(1)} %bitcast_dynamic-update-slice_fusion.4, bf16[2,128,256]{2,0,1:T(2,128)(2,1)} %collective-permute-done.8), kind=kLoop, calls=%fused_computation.11 | loop fusion | bytes 262144
  74.4 1.0 %bitcast_dynamic-update-slice_fusion.1 = bf16[6,2,128,256]{3,1,2,0:T(2,128)(2,1)S(1)} fusion(bf16[6,2,128,256]{3,1,2,0:T(2,128)(2,1)S(1)} %bitcast_dynamic-update-slice_fusion.2, bf16[2,128,256]{2,0,1:T(2,128)(2,1)} %collective-permute-done.10), kind=kLoop, calls=%fused_computation.9 | loop fusion | bytes 262144
  75.4 7.7 %collective-permute-done.11 = bf16[2,128,256]{2,0,1:T(2,128)(2,1)S(1)} collective-permute-done((bf16[2,128,256]{2,0,1:T(2,128)(2,1)S(1)}, bf16[2,128,256]{2,0,1:T(2,128)(2,1)S(1)}, u32[]{:S(2)}, u32[]{:S(2)}) %collective-permute-start.11) | collective-permute-done | bytes 131104 | tf_op jit(solution)/shard_map/ppermute | solution.py:15
  83.2 1.0 %convolution_convert_fusion.1 = bf16[2,4,128,256]{3,1,2,0:T(4,128)(2,1)S(1)} fusion(bf16[6,2,128,256]{3,1,2,0:T(2,128)(2,1)S(1)} %bitcast_dynamic-update-slice_fusion, f32[2,6]{1,0:T(2,128)S(1)} %convert_bitcast_fusion, f32[4]{0:T(128)S(1)} %add_convert_fusion), kind=kOutput, calls=%fused_computation.1 | convolution fusion | flops 3407920 | bytes 1310784 | tf_op jit(solution)/shard_map/kjs,skfr->kjfr/dot_general | solution.py:166
  84.4 11.5 %shard_map.64 = f32[2,512,256]{2,1,0:T(8,128)} custom-call(bf16[2,512,256]{2,1,0:T(8,128)(2,1)S(1)} %bitcast.42), custom_call_target="tpu_custom_call" | custom-call | tf_op jit(solution)/shard_map/pallas_call | solution.py:106
  (30 shorter events, 0.9 us)
Async XLA Ops:
  0.0 1.8 %copy-start = (bf16[5,128,2048]{2,1,0:T(8,128)(2,1)S(1)}, bf16[5,128,2048]{2,1,0:T(8,128)(2,1)}, u32[]{:S(2)}) copy-start(bf16[5,128,2048]{2,1,0:T(8,128)(2,1)} %param.6) | copy-start | bytes 7864324
  1.8 23.9 %copy-start.1 = (s32[64]{0:T(128)S(1)}, s32[64]{0:T(128)}, u32[]{:S(2)}) copy-start(s32[64]{0:T(128)} %param.11) | copy-start | bytes 772
  1.8 23.9 %copy-start.2 = (s32[5]{0:T(128)S(1)}, s32[5]{0:T(128)}, u32[]{:S(2)}) copy-start(s32[5]{0:T(128)} %param.8) | copy-start | bytes 64
  4.7 35.7 %copy-start.3 = (s32[5]{0:T(128)S(1)}, s32[5]{0:T(128)}, u32[]{:S(2)}) copy-start(s32[5]{0:T(128)} %param.9) | copy-start | bytes 64
  27.1 44.1 %collective-permute-start.6 = (bf16[2,128,256]{2,0,1:T(2,128)(2,1)S(1)}, bf16[2,128,256]{2,0,1:T(2,128)(2,1)}, u32[]{:S(2)}, u32[]{:S(2)}) collective-permute-start(bf16[2,128,256]{2,0,1:T(2,128)(2,1)S(1)} %get-tuple-element.12), channel_id=1, source_target_pairs={{12,0},{16,4},{20,8},{24,12},{28,16},{32,20},{36,24},{40,28},{44,3... | collective-permute-start | bytes 393224 | tf_op jit(solution)/shard_map/ppermute | solution.py:15
  39.9 32.3 %collective-permute-start.7 = (bf16[2,128,256]{2,0,1:T(2,128)(2,1)S(1)}, bf16[2,128,256]{2,0,1:T(2,128)(2,1)}, u32[]{:S(2)}, u32[]{:S(2)}) collective-permute-start(bf16[2,128,256]{2,0,1:T(2,128)(2,1)S(1)} %get-tuple-element.11), channel_id=1, source_target_pairs={{8,0},{12,4},{16,8},{20,12},{24,16},{28,20},{32,24},{36,28},{40,32... | collective-permute-start | bytes 393224 | tf_op jit(solution)/shard_map/ppermute | solution.py:15
  40.3 32.9 %collective-permute-start.8 = (bf16[2,128,256]{2,0,1:T(2,128)(2,1)S(1)}, bf16[2,128,256]{2,0,1:T(2,128)(2,1)}, u32[]{:S(2)}, u32[]{:S(2)}) collective-permute-start(bf16[2,128,256]{2,0,1:T(2,128)(2,1)S(1)} %get-tuple-element.10), channel_id=1, source_target_pairs={{4,0},{8,4},{12,8},{16,12},{20,16},{24,20},{28,24},{32,28},{36,32}... | collective-permute-start | bytes 393224 | tf_op jit(solution)/shard_map/ppermute | solution.py:15
  40.3 33.9 %collective-permute-start.9 = (bf16[2,128,256]{2,0,1:T(2,128)(2,1)S(1)}, bf16[2,128,256]{2,0,1:T(2,128)(2,1)S(1)}, u32[]{:S(2)}, u32[]{:S(2)}) collective-permute-start(bf16[2,128,256]{2,0,1:T(2,128)(2,1)S(1)} %get-tuple-element.9), channel_id=1, source_target_pairs={{0,0},{4,4},{8,8},{12,12},{16,16},{20,20},{24,24},{28,28},{32,32},... | collective-permute-start | bytes 393224 | tf_op jit(solution)/shard_map/ppermute | solution.py:15
  41.2 4.5 %collective-permute-start = (bf16[2]{0:T(256)(128)(2,1)S(1)}, bf16[2]{0:T(256)(128)(2,1)S(1)}, u32[]{:S(2)}, u32[]{:S(2)}) collective-permute-start(bf16[2]{0:T(256)(128)(2,1)S(1)} %get-tuple-element.18), channel_id=1, source_target_pairs={{12,0},{16,4},{20,8},{24,12},{28,16},{32,20},{36,24},{40,28},{44,3... | collective-permute-start | bytes 20 | tf_op jit(solution)/shard_map/ppermute | solution.py:15
  45.7 3.0 %copy-start.4 = (bf16[2]{0:T(256)(128)(2,1)}, bf16[2]{0:T(256)(128)(2,1)S(1)}, u32[]{:S(2)}) copy-start(bf16[2]{0:T(256)(128)(2,1)S(1)} %collective-permute-done) | copy-start | bytes 16
  45.7 3.9 %collective-permute-start.1 = (bf16[2]{0:T(256)(128)(2,1)}, bf16[2]{0:T(256)(128)(2,1)}, u32[]{:S(2)}, u32[]{:S(2)}) collective-permute-start(bf16[2]{0:T(256)(128)(2,1)} %get-tuple-element.17), channel_id=1, source_target_pairs={{8,0},{12,4},{16,8},{20,12},{24,16},{28,20},{32,24},{36,28},{40,32... | collective-permute-start | bytes 20 | tf_op jit(solution)/shard_map/ppermute | solution.py:15
  49.6 4.6 %collective-permute-start.2 = (bf16[2]{0:T(256)(128)(2,1)}, bf16[2]{0:T(256)(128)(2,1)}, u32[]{:S(2)}, u32[]{:S(2)}) collective-permute-start(bf16[2]{0:T(256)(128)(2,1)} %get-tuple-element.16), channel_id=1, source_target_pairs={{4,0},{8,4},{12,8},{16,12},{20,16},{24,20},{28,24},{32,28},{36,32}... | collective-permute-start | bytes 20 | tf_op jit(solution)/shard_map/ppermute | solution.py:15
  54.2 2.5 %collective-permute-start.3 = (bf16[2]{0:T(256)(128)(2,1)}, bf16[2]{0:T(256)(128)(2,1)}, u32[]{:S(2)}, u32[]{:S(2)}) collective-permute-start(bf16[2]{0:T(256)(128)(2,1)} %get-tuple-element.15), channel_id=1, source_target_pairs={{0,0},{4,4},{8,8},{12,12},{16,16},{20,20},{24,24},{28,28},{32,32},... | collective-permute-start | bytes 20 | tf_op jit(solution)/shard_map/ppermute | solution.py:15
  56.7 3.0 %collective-permute-start.4 = (bf16[2]{0:T(256)(128)(2,1)S(1)}, bf16[2]{0:T(256)(128)(2,1)}, u32[]{:S(2)}, u32[]{:S(2)}) collective-permute-start(bf16[2]{0:T(256)(128)(2,1)S(1)} %get-tuple-element.14), channel_id=1, source_target_pairs={{252,0},{0,4},{4,8},{8,12},{12,16},{16,20},{20,24},{24,28},{28,32}... | collective-permute-start | bytes 20 | tf_op jit(solution)/shard_map/ppermute | solution.py:15
  59.7 6.2 %collective-permute-start.5 = (bf16[2]{0:T(256)(128)(2,1)S(1)}, bf16[2]{0:T(256)(128)(2,1)}, u32[]{:S(2)}, u32[]{:S(2)}) collective-permute-start(bf16[2]{0:T(256)(128)(2,1)S(1)} %get-tuple-element.13), channel_id=1, source_target_pairs={{248,0},{252,4},{0,8},{4,12},{8,16},{12,20},{16,24},{20,28},{24,32... | collective-permute-start | bytes 20 | tf_op jit(solution)/shard_map/ppermute | solution.py:15
  65.9 8.5 %collective-permute-start.10 = (bf16[2,128,256]{2,0,1:T(2,128)(2,1)S(1)}, bf16[2,128,256]{2,0,1:T(2,128)(2,1)}, u32[]{:S(2)}, u32[]{:S(2)}) collective-permute-start(bf16[2,128,256]{2,0,1:T(2,128)(2,1)S(1)} %get-tuple-element.8), channel_id=1, source_target_pairs={{252,0},{0,4},{4,8},{8,12},{12,16},{16,20},{20,24},{24,28},{28,32}... | collective-permute-start | bytes 393224 | tf_op jit(solution)/shard_map/ppermute | solution.py:15
  71.2 11.9 %collective-permute-start.11 = (bf16[2,128,256]{2,0,1:T(2,128)(2,1)S(1)}, bf16[2,128,256]{2,0,1:T(2,128)(2,1)S(1)}, u32[]{:S(2)}, u32[]{:S(2)}) collective-permute-start(bf16[2,128,256]{2,0,1:T(2,128)(2,1)S(1)} %get-tuple-element.7), channel_id=1, source_target_pairs={{248,0},{252,4},{0,8},{4,12},{8,16},{12,20},{16,24},{20,28},{24,32... | collective-permute-start | bytes 393224 | tf_op jit(solution)/shard_map/ppermute | solution.py:15

commit v2 on v0

v2 whole, which is shorter than its diff:
```python
import jax
import jax.numpy as jnp
from jax import lax
from jax.experimental import pallas as pl
from jax.experimental.pallas import tpu as pltpu
from jax.sharding import PartitionSpec as P

FACES = 4
QUARTERS = 4
SPAN = 5
B = 64
HI = lax.Precision.HIGHEST
f32 = jnp.float32
bf16 = jnp.bfloat16
VM = pl.BlockSpec(memory_space=pltpu.VMEM)
SM = pl.BlockSpec(memory_space=pltpu.SMEM)
ANY = pl.BlockSpec(memory_space=pl.ANY)
PARAMS = pltpu.CompilerParams(vmem_limit_bytes=40 << 20)
ROUTES = (1, -1, -2, 2, -3)


def shifted(block, axis, distance):
    n = lax.axis_size(axis)
    return lax.ppermute(block, axis, [(i, (i + distance) % n) for i in range(n)])


def mm(a, b, dims=((1,), (0,)), prec=HI):
    return lax.dot_general(a, b, (dims, ((), ())), precision=prec, preferred_element_type=f32)


def sketch_kernel(t_hbm, r_hbm, o0, o1, o2, o3, t, r, sem):
    s = lax.axis_index("samp")
    outs = (o0, o1, o2, o3)
    slots, rows = o0.shape[0], o0.shape[1]
    order = (2, 1, 3, 0)
    load_r = pltpu.make_async_copy(r_hbm, r, sem.at[4])
    load_r.start()
    loads = []
    for k in order:
        c = lax.rem(s + k, QUARTERS)
        load = pltpu.make_async_copy(
            t_hbm.at[:, pl.ds(pl.multiple_of(c * rows, rows), rows), :], t.at[k], sem.at[k]
        )
        load.start()
        loads.append(load)
    load_r.wait()
    for k, load in zip(order, loads):
        load.wait()
        x = t[k].reshape(slots * rows, t.shape[3])
        y = mm(x, r[...], prec=None)
        outs[k][...] = y.reshape(outs[k].shape)


def sketch_parts(traces, sketch):
    slots, cells, samples = traces.shape
    rows = cells // QUARTERS
    rank = sketch.shape[1]
    part = jax.ShapeDtypeStruct((slots, rows, rank), f32)
    return pl.pallas_call(
        sketch_kernel,
        out_shape=[part] * QUARTERS,
        in_specs=[ANY, ANY],
        out_specs=[VM] * QUARTERS,
        scratch_shapes=[
            pltpu.VMEM((QUARTERS, slots, rows, samples), bf16),
            pltpu.VMEM((samples, rank), bf16),
            pltpu.SemaphoreType.DMA((QUARTERS + 1,)),
        ],
        compiler_params=PARAMS,
    )(traces, sketch)


def place_kernel(port, count, owner, a, b, c, d, p1, m1, m2, p2, m3, here, total):
    me = lax.axis_index("mesh")
    n = owner.shape[0]
    total[...] = ((a[...] + b[...]) + (c[...] + d[...])).astype(bf16)
    sends = {}
    for dist in range(SPAN):
        p = lax.rem(me - dist + n, n)
        lean = lax.rem(owner[p] - p + n, n)
        slot = jnp.int32(-1)
        for i in range(total.shape[0]):
            slot = jnp.where((port[i] == p) & (i < count[0]), i, slot)
        sends[dist] = (slot, lean)

    def tile(dist, lean):
        slot, its = sends[dist]
        good = (slot >= 0) & (its == lean)
        return jnp.where(good, total[jnp.maximum(slot, 0)], jnp.inf).astype(bf16)

    for out, near in ((p1, 0), (here, 1), (m1, 2), (m2, 3)):
        out[0] = tile(near, 1)
        out[1] = tile(near + 1, 2)
    p2[0] = tile(0, 2)
    m3[0] = tile(4, 1)


def place(face_port, tile_count, port_owner, parts):
    slots, rows, rank = parts[0].shape
    two = jax.ShapeDtypeStruct((2, rows, rank), bf16)
    one = jax.ShapeDtypeStruct((1, rows, rank), bf16)
    return pl.pallas_call(
        place_kernel,
        out_shape=[two, two, two, one, one, two],
        in_specs=[SM] * 3 + [VM] * 4,
        out_specs=[VM] * 6,
        scratch_shapes=[pltpu.VMEM((slots, rows, rank), bf16)],
        compiler_params=PARAMS,
    )(face_port, tile_count, port_owner, *parts)


def pick_kernel(p1, m1, m2, p2, m3, here, out):
    near = [p1[0], here[0], m1[0], m2[0], m3[0]]
    far = [p2[0], p1[1], here[1], m1[1], m2[1]]
    for lean, tiles in enumerate((near, far)):
        tiles = [t.astype(f32) for t in tiles]
        full = [t < jnp.inf for t in tiles]
        run = full[0]
        for j in range(FACES):
            if j:
                run = run & full[j]
            x = jnp.where(run, tiles[j], tiles[j + 1])
            out[lean, j] = jnp.where(x < jnp.inf, x, 0.0).astype(bf16)


def pick(tiles):
    rows, rank = tiles[0].shape[1:]
    return pl.pallas_call(
        pick_kernel,
        out_shape=jax.ShapeDtypeStruct((2, FACES, rows, rank), bf16),
        in_specs=[VM] * 6,
        out_specs=VM,
        compiler_params=PARAMS,
    )(*tiles)


def panel(t0):
    lane = lax.broadcasted_iota(jnp.int32, (B, 128), 1)
    row = lax.broadcasted_iota(jnp.int32, (B, 128), 0)
    t1 = ((lane % B) == row).astype(f32)
    half = jnp.where(lane < B, 0, B)
    groups = B // 8
    r0 = [t0[8 * i : 8 * i + 8] for i in range(groups)]
    r1 = [t1[8 * i : 8 * i + 8] for i in range(groups)]
    h8, row8 = half[:8], row[:8]
    done = []
    for g in range(groups):
        n = groups - g
        cols = [
            [
                jnp.take_along_axis(r0[g + i], h8 + (8 * g + j), axis=1, mode="promise_in_bounds")
                for i in range(n)
            ]
            for j in range(8)
        ]
        for j in range(0, 8, 2):
            cj, ck = cols[j], cols[j + 1]
            a, b, d = cj[0][j : j + 1], cj[0][j + 1 : j + 2], ck[0][j + 1 : j + 2]
            inv = 1.0 / (a * d - b * b)
            i00, i01, i11 = d * inv, -b * inv, a * inv
            m0 = [x * i00 + y * i01 for x, y in zip(cj, ck)]
            m1 = [x * i01 + y * i11 for x, y in zip(cj, ck)]
            keep = row8 > j + 1
            m0[0] = jnp.where(keep, m0[0], 0.0)
            m1[0] = jnp.where(keep, m1[0], 0.0)
            for k in range(j + 2, 8):
                p, q = cols[k][0][j : j + 1], cols[k][0][j + 1 : j + 2]
                cols[k] = [c - (x * p + y * q) for c, x, y in zip(cols[k], m0, m1)]
            p0, q0 = r0[g][j : j + 1], r0[g][j + 1 : j + 2]
            p1, q1 = r1[g][j : j + 1], r1[g][j + 1 : j + 2]
            done.append((a, b, d, p1, q1))
            for i in range(n):
                if i > 0 or j < 6:
                    r0[g + i] = r0[g + i] - (m0[i] * p0 + m1[i] * q0)
                r1[g + i] = r1[g + i] - (m0[i] * p1 + m1[i] * q1)
    rows = []
    for a, b, d, p1, q1 in done:
        l10 = b * (1.0 / a)
        rows.append(p1 * lax.rsqrt(a))
        rows.append((q1 - l10 * p1) * lax.rsqrt(d - b * l10))
    return jnp.concatenate(rows, axis=0)


def solve_kernel(owner, x0, x1, x2, x3, o_ref, x_ref, s_ref):
    me = lax.axis_index("mesh")
    s = lax.axis_index("samp")
    ports = owner.shape[0]
    near, far = lax.rem(me - 1 + ports, ports), lax.rem(me - 2 + ports, ports)
    both = (owner[near] == me) & (owner[far] == me)
    near_first = jnp.where(both, near < far, owner[near] == me)
    slots = (jnp.where(near_first, 0, 1), jnp.where(near_first, 1, 0))
    n = x0.shape[3]
    rows = x0.shape[2]
    each = FACES * rows
    row = lax.broadcasted_iota(jnp.int32, (n, n), 0)
    col = lax.broadcasted_iota(jnp.int32, (n, n), 1)
    eye = (row == col).astype(f32)
    for p in range(2):
        for k, x in enumerate((x0, x1, x2, x3)):
            x_ref[p, k * each : (k + 1) * each] = x[p].reshape(each, n)
        x = x_ref[p]
        g = mm(x, x, ((0,), (0,)), None)
        s_ref[p] = g + (0.1 * jnp.sum(g * eye) / n + 1e-6) * eye
    for k in range(n // B):
        lo, hi = k * B, (k + 1) * B
        t = panel(jnp.concatenate([s_ref[0, lo:hi, lo:hi], s_ref[1, lo:hi, lo:hi]], axis=1))
        for p in range(2):
            w = t[:, p * B : (p + 1) * B]
            c = col[:B]
            inside = (c >= lo) & (c < hi)
            sk = jnp.where(inside, (c - lo == row[:B]).astype(f32), s_ref[p, lo:hi, :])
            y = mm(w, sk)
            if hi < n:
                u = mm(s_ref[p, hi:, lo:hi], w, ((1,), (1,)))
                c = col[hi:]
                old = jnp.where((c >= lo) & (c < hi), 0.0, s_ref[p, hi:, :])
                s_ref[p, hi:, :] = old - mm(u, y)
            s_ref[p, lo:hi, :] = y
    for p in range(2):
        w = jnp.where(col <= row, s_ref[p], 0.0)
        w0 = w.astype(bf16)
        e = w - w0.astype(f32)
        w1 = e.astype(bf16)
        w2 = (e - w1.astype(f32)).astype(bf16)
        x = x_ref[p]
        acc = mm(x, w2, ((1,), (1,)), None) + mm(x, w1, ((1,), (1,)), None)
        y = acc + mm(x, w0, ((1,), (1,)), None)
        for k in range(QUARTERS):
            q = lax.rem(s - k + QUARTERS, QUARTERS)
            for j in range(FACES):
                at = pl.multiple_of(j * QUARTERS * rows + q * rows, rows)
                o_ref[slots[p], pl.ds(at, rows), :] = y[k * each + j * rows : k * each + (j + 1) * rows]


def solve(port_owner, pieces):
    rows, n = pieces[0].shape[2:]
    height = FACES * QUARTERS * rows
    return pl.pallas_call(
        solve_kernel,
        out_shape=jax.ShapeDtypeStruct((2, height, n), f32),
        in_specs=[SM] + [VM] * QUARTERS,
        out_specs=VM,
        scratch_shapes=[pltpu.VMEM((2, height, n), bf16), pltpu.VMEM((2, n, n), f32)],
        compiler_params=PARAMS,
    )(port_owner, *pieces)


def body(traces, sketch, face_port, face_pos, tile_count, port_owner):
    own, k1, k2, k3 = sketch_parts(traces, sketch)
    k2 = shifted(k2, "samp", 2)
    k1 = shifted(k1, "samp", 1)
    k3 = shifted(k3, "samp", -1)
    *sends, here = place(face_port, tile_count, port_owner, (own, k1, k2, k3))
    tiles = [shifted(x, "mesh", distance) for x, distance in zip(sends, ROUTES)]
    mine = pick((*tiles, here))
    pieces = [mine] + [shifted(mine, "samp", k) for k in range(1, QUARTERS)]
    return solve(port_owner, pieces)


def solution(mesh):
    placed = (P("mesh", None, "samp"), P("samp", None), P("mesh"), P("mesh"), P("mesh"), P())
    return jax.shard_map(
        body, mesh=mesh, in_specs=placed, out_specs=P("mesh", None, None), check_vma=False
    )
```

time: 224 us -> 58.1 us (0.26)
  other arithmetic: 120 us -> 0 us
  local copies, waits for them, and re-layouts: 29.7 us -> 2.97 us
  blocking collectives: 21 us -> 0 us
  Pallas kernels: 0 us -> 15 us
  matrix products: 13.9 us -> 0 us
    another operation x15 -> x0, other arithmetic: 113 us -> none  [the longest x10 69.6 us: orthonormal(): jnp.linalg.cholesky(gram_matrix + diagonal_shift * jnp.eye(rank_width, dt...]
    psum x1 -> x0, blocking collectives: 21 us -> none  [body(): summed = lax.psum(partial_sum, 'samp').astype(jnp.bfloat16)]
    another operation x18 -> x0, local copies, waits for them, and re-layouts: 19.7 us -> none  [the longest x7 8.94 us: route_whole(): jnp.stack([pair[1] for pair in arrived])]
    pallas_call x0 -> x4, Pallas kernels: none -> 15 us  [the longest x1 12 us: solve(): pl.pallas_call(solve_kernel, out_shape=jax.ShapeDtypeStruct((2, height, n...]
    dot_general x5 -> x0, matrix products: 7.11 us -> none  [the longest x1 2.93 us: body(): jnp.einsum('sfk,kr->sfr', traces, sketch, preferred_element_type=jnp.floa...]
    another operation x5 -> x0, matrix products: 6.78 us -> none  [the longest x2 3.84 us: orthonormal(): jnp.linalg.cholesky(gram_matrix + diagonal_shift * jnp.eye(rank_width, dt...]
    unnamed x19 -> x8, local copies, waits for them, and re-layouts: 5.94 us -> 2.97 us
    ppermute x12 -> x11, starting transfers between devices: 23.8 us -> 25.6 us  [shifted(): lax.ppermute(block, axis, [(i, (i + distance) % n) for i in range(n)])]
  transfers between devices with their start and end apart: 12 -> 11, of which waited for: 4 -> 5; matrix products, arithmetic and copies ran while one was open for 8% -> 0% of each run, Pallas kernels for 0% -> 0%
where the time goes in v2:
time: 58.1 us; the launch traced here: 57.9 us
  starting transfers between devices  25.6 us (44%)
  Pallas kernels  15 us (26%)
  waiting for transfers between devices  13.7 us (24%)
  local copies, waits for them, and re-layouts  2.97 us (5%)
  between operations  0.7 us (1%)
    ppermute x11, starting transfers between devices, shifted(): lax.ppermute(block, axis, [(i, (i + distance) % n) for i in range(n)])  25.6 us
    ppermute x11, waiting for transfers between devices, shifted(): lax.ppermute(block, axis, [(i, (i + distance) % n) for i in range(n)])  13.7 us
    pallas_call x1, Pallas kernels, solve(): pl.pallas_call(solve_kernel, out_shape=jax.ShapeDtypeStruct((2, height, n...  12 us
    unnamed x8, local copies, waits for them, and re-layouts  2.97 us
    pallas_call x1, Pallas kernels, sketch_parts(): pl.pallas_call(sketch_kernel, out_shape=[part] * QUARTERS, in_specs=[ANY,...  2.25 us
  transfers between devices with their start and end apart: 11, of which 5 were waited for; matrix products, arithmetic and copies ran while one was open for 0% of the time, Pallas kernels for 0%

profile of v2, /device:TPU:1, one launch (start us, length us, event | category | flops | bytes accessed | tf_op | source)
XLA Modules:
  0.0 57.9 jit_solution(1777771425488306529)
XLA Ops:
  0.0 0.0 copy-start
  0.0 1.7 %copy-done = bf16[5,128,2048]{2,1,0:T(8,128)(2,1)S(1)} copy-done((bf16[5,128,2048]{2,1,0:T(8,128)(2,1)S(1)}, bf16[5,128,2048]{2,1,0:T(8,128)(2,1)}, u32[]{:S(2)}) %copy-start) | copy-done | bytes 2621464
  1.7 0.0 copy-start.1
  1.7 1.2 %copy-done.1 = bf16[2048,256]{1,0:T(8,128)(2,1)S(1)} copy-done((bf16[2048,256]{1,0:T(8,128)(2,1)S(1)}, bf16[2048,256]{1,0:T(8,128)(2,1)}, u32[]{:S(2)}) %copy-start.1) | copy-done | bytes 1048600
  3.0 2.3 %shard_map.55 = (f32[5,32,256]{2,1,0:T(8,128)S(1)}, f32[5,32,256]{2,1,0:T(8,128)S(1)}, f32[5,32,256]{2,1,0:T(8,128)S(1)}, f32[5,32,256]{2,1,0:T(8,128)S(1)}) custom-call(bf16[5,128,2048]{2,1,0:T(8,128)(2,1)S(1)} %copy-done, bf16[2048,256]{1,0:T(8,128)(2,1)S(1)} %copy-done.1), custom_call_target="tpu_custom_call" | custom-call | tf_op jit(solution)/shard_map/pallas_call | solution.py:59
  5.2 2.1 %collective-permute-start = (f32[5,32,256]{2,1,0:T(8,128)S(1)}, f32[5,32,256]{2,1,0:T(8,128)S(1)}, u32[]{:S(2)}, u32[]{:S(2)}) collective-permute-start(f32[5,32,256]{2,1,0:T(8,128)S(1)} %get-tuple-element.16), channel_id=1, source_target_pairs={{0,1},{1,2},{2,3},{3,0},{4,5},{5,6},{6,7},{7,4},{8,9},{9,10},{10,1... | collective-permute-start | bytes 491528 | tf_op jit(solution)/shard_map/ppermute | solution.py:24
  7.3 2.4 %collective-permute-start.1 = (f32[5,32,256]{2,1,0:T(8,128)S(1)}, f32[5,32,256]{2,1,0:T(8,128)S(1)}, u32[]{:S(2)}, u32[]{:S(2)}) collective-permute-start(f32[5,32,256]{2,1,0:T(8,128)S(1)} %get-tuple-element.17), channel_id=1, source_target_pairs={{0,2},{1,3},{2,0},{3,1},{4,6},{5,7},{6,4},{7,5},{8,10},{9,11},{10,... | collective-permute-start | bytes 491528 | tf_op jit(solution)/shard_map/ppermute | solution.py:24
  9.8 1.2 %collective-permute-start.2 = (f32[5,32,256]{2,1,0:T(8,128)S(1)}, f32[5,32,256]{2,1,0:T(8,128)S(1)}, u32[]{:S(2)}, u32[]{:S(2)}) collective-permute-start(f32[5,32,256]{2,1,0:T(8,128)S(1)} %get-tuple-element.18), channel_id=1, source_target_pairs={{0,3},{1,0},{2,1},{3,2},{4,7},{5,4},{6,5},{7,6},{8,11},{9,8},{10,9... | collective-permute-start | bytes 491528 | tf_op jit(solution)/shard_map/ppermute | solution.py:24
  11.6 0.0 collective-permute-done.b
  11.6 5.3 %collective-permute-done.1.c = f32[5,32,256]{2,1,0:T(8,128)S(1)} collective-permute-done((f32[5,32,256]{2,1,0:T(8,128)S(1)}, f32[5,32,256]{2,1,0:T(8,128)S(1)}, u32[]{:S(2)}, u32[]{:S(2)}) %collective-permute-start.1) | collective-permute-done | bytes 163872 | tf_op jit(solution)/shard_map/ppermute | solution.py:24
  17.0 0.0 collective-permute-done.2.d
  17.0 0.0 copy-done.2
  17.0 0.0 copy-done.3
  17.0 0.6 %shard_map.56 = (bf16[2,32,256]{2,1,0:T(8,128)(2,1)S(1)}, bf16[2,32,256]{2,1,0:T(8,128)(2,1)S(1)}, bf16[2,32,256]{2,1,0:T(8,128)(2,1)S(1)}, bf16[1,32,256]{2,1,0...) custom-call(s32[5]{0:T(128)S(1)} %copy-done.3, s32[1]{0:T(128)S(6)} %copy.6.count, ...), custom_call_target="tpu_custom_call" | custom-call | tf_op jit(solution)/shard_map/pallas_call | solution.py:102
  17.6 2.8 %collective-permute-start.3 = (bf16[2,32,256]{2,1,0:T(8,128)(2,1)S(1)}, bf16[2,32,256]{2,1,0:T(8,128)(2,1)S(1)}, u32[]{:S(2)}, u32[]{:S(2)}) collective-permute-start(bf16[2,32,256]{2,1,0:T(8,128)(2,1)S(1)} %get-tuple-element.19), channel_id=1, source_target_pairs={{0,4},{4,8},{8,12},{12,16},{16,20},{20,24},{24,28},{28,32},{32,36}... | collective-permute-start | bytes 98312 | tf_op jit(solution)/shard_map/ppermute | solution.py:24
  20.4 0.0 collective-permute-start.4
  20.4 6.9 %collective-permute-start.5 = (bf16[2,32,256]{2,1,0:T(8,128)(2,1)S(1)}, bf16[2,32,256]{2,1,0:T(8,128)(2,1)S(1)}, u32[]{:S(2)}, u32[]{:S(2)}) collective-permute-start(bf16[2,32,256]{2,1,0:T(8,128)(2,1)S(1)} %get-tuple-element.21), channel_id=1, source_target_pairs={{0,248},{4,252},{8,0},{12,4},{16,8},{20,12},{24,16},{28,20},{32,24... | collective-permute-start | bytes 98312 | tf_op jit(solution)/shard_map/ppermute | solution.py:24
  27.3 0.0 collective-permute-start.6
  27.3 6.9 %collective-permute-start.7 = (bf16[1,32,256]{2,1,0:T(8,128)(2,1)S(1)}, bf16[1,32,256]{2,1,0:T(8,128)(2,1)S(1)}, u32[]{:S(2)}, u32[]{:S(2)}) collective-permute-start(bf16[1,32,256]{2,1,0:T(8,128)(2,1)S(1)} %get-tuple-element.23), channel_id=1, source_target_pairs={{0,244},{4,248},{8,252},{12,0},{16,4},{20,8},{24,12},{28,16},{32,2... | collective-permute-start | bytes 49160 | tf_op jit(solution)/shard_map/ppermute | solution.py:24
  34.2 0.0 collective-permute-done.6.p2
  34.2 0.9 %collective-permute-done.7.m3 = bf16[1,32,256]{2,1,0:T(8,128)(2,1)S(1)} collective-permute-done((bf16[1,32,256]{2,1,0:T(8,128)(2,1)S(1)}, bf16[1,32,256]{2,1,0:T(8,128)(2,1)S(1)}, u32[]{:S(2)}, u32[]{:S(2)}) %collective-permute-start.7) | collective-permute-done | bytes 16416 | tf_op jit(solution)/shard_map/ppermute | solution.py:24
  35.1 0.0 collective-permute-done.3.p1
  35.1 0.0 collective-permute-done.4.m1
  35.1 0.0 collective-permute-done.5.m2
  35.1 0.1 shard_map.57.x0
  35.1 2.1 %collective-permute-start.10 = (bf16[2,4,32,256]{3,2,1,0:T(8,128)(2,1)S(1)}, bf16[2,4,32,256]{3,2,1,0:T(8,128)(2,1)S(1)}, u32[]{:S(2)}, u32[]{:S(2)}) collective-permute-start(bf16[2,4,32,256]{3,2,1,0:T(8,128)(2,1)S(1)} %shard_map.57.x0), channel_id=1, source_target_pairs={{0,3},{1,0},{2,1},{3,2},{4,7},{5,4},{6,5},{7,6},{8,11},{9,8},{10,9... | collective-permute-start | bytes 393224 | tf_op jit(solution)/shard_map/ppermute | solution.py:24
  37.2 0.9 %collective-permute-start.9 = (bf16[2,4,32,256]{3,2,1,0:T(8,128)(2,1)S(1)}, bf16[2,4,32,256]{3,2,1,0:T(8,128)(2,1)S(1)}, u32[]{:S(2)}, u32[]{:S(2)}) collective-permute-start(bf16[2,4,32,256]{3,2,1,0:T(8,128)(2,1)S(1)} %shard_map.57.x0), channel_id=1, source_target_pairs={{0,2},{1,3},{2,0},{3,1},{4,6},{5,7},{6,4},{7,5},{8,10},{9,11},{10,... | collective-permute-start | bytes 393224 | tf_op jit(solution)/shard_map/ppermute | solution.py:24
  38.0 0.4 collective-permute-start.8
  38.4 0.9 %collective-permute-done.10.x3 = bf16[2,4,32,256]{3,2,1,0:T(8,128)(2,1)S(1)} collective-permute-done((bf16[2,4,32,256]{3,2,1,0:T(8,128)(2,1)S(1)}, bf16[2,4,32,256]{3,2,1,0:T(8,128)(2,1)S(1)}, u32[]{:S(2)}, u32[]{:S(2)}) %collective-permute-start.10) | collective-permute-done | bytes 131104 | tf_op jit(solution)/shard_map/ppermute | solution.py:24
  39.4 3.2 %collective-permute-done.9.x2 = bf16[2,4,32,256]{3,2,1,0:T(8,128)(2,1)S(1)} collective-permute-done((bf16[2,4,32,256]{3,2,1,0:T(8,128)(2,1)S(1)}, bf16[2,4,32,256]{3,2,1,0:T(8,128)(2,1)S(1)}, u32[]{:S(2)}, u32[]{:S(2)}) %collective-permute-start.9) | collective-permute-done | bytes 131104 | tf_op jit(solution)/shard_map/ppermute | solution.py:24
  42.6 3.3 %collective-permute-done.8.x1 = bf16[2,4,32,256]{3,2,1,0:T(8,128)(2,1)S(1)} collective-permute-done((bf16[2,4,32,256]{3,2,1,0:T(8,128)(2,1)S(1)}, bf16[2,4,32,256]{3,2,1,0:T(8,128)(2,1)S(1)}, u32[]{:S(2)}, u32[]{:S(2)}) %collective-permute-start.8) | collective-permute-done | bytes 131104 | tf_op jit(solution)/shard_map/ppermute | solution.py:24
  45.9 12.0 %shard_map.58 = f32[2,512,256]{2,1,0:T(8,128)} custom-call(s32[64]{0:T(128)S(1)} %copy-done.2, bf16[2,4,32,256]{3,2,1,0:T(8,128)(2,1)S(1)} %shard_map.57.x0, bf16[2,4,32,256]{3,2,1,0:T(8,128)(2,1)S(1)} %collective-permute-done.8.x1, bf16[2,4,32,256]{3,2,1,0:T(8,128)(2,1)S(1)} %collective-permute-done.9.x2, bf16[2,4,32,256]{3,2,1,0:T(8,128)(2,1)S(1)} %collective-permute-done.10.x3), custom_call_target="tpu_custom_call" | custom-call | tf_op jit(solution)/shard_map/pallas_call | solution.py:238
  (2 shorter events, 0.0 us)
Async XLA Ops:
  0.0 1.7 %copy-start = (bf16[5,128,2048]{2,1,0:T(8,128)(2,1)S(1)}, bf16[5,128,2048]{2,1,0:T(8,128)(2,1)}, u32[]{:S(2)}) copy-start(bf16[5,128,2048]{2,1,0:T(8,128)(2,1)} %t_hbm.1) | copy-start | bytes 7864324
  1.7 1.2 %copy-start.1 = (bf16[2048,256]{1,0:T(8,128)(2,1)S(1)}, bf16[2048,256]{1,0:T(8,128)(2,1)}, u32[]{:S(2)}) copy-start(bf16[2048,256]{1,0:T(8,128)(2,1)} %r_hbm.1) | copy-start | bytes 3145732
  3.0 14.0 %copy-start.2 = (s32[64]{0:T(128)S(1)}, s32[64]{0:T(128)}, u32[]{:S(2)}) copy-start(s32[64]{0:T(128)} %owner.3) | copy-start | bytes 772
  3.0 14.0 %copy-start.3 = (s32[5]{0:T(128)S(1)}, s32[5]{0:T(128)}, u32[]{:S(2)}) copy-start(s32[5]{0:T(128)} %port.1) | copy-start | bytes 64
  5.2 6.4 %collective-permute-start = (f32[5,32,256]{2,1,0:T(8,128)S(1)}, f32[5,32,256]{2,1,0:T(8,128)S(1)}, u32[]{:S(2)}, u32[]{:S(2)}) collective-permute-start(f32[5,32,256]{2,1,0:T(8,128)S(1)} %get-tuple-element.16), channel_id=1, source_target_pairs={{0,1},{1,2},{2,3},{3,0},{4,5},{5,6},{6,7},{7,4},{8,9},{9,10},{10,1... | collective-permute-start | bytes 491528 | tf_op jit(solution)/shard_map/ppermute | solution.py:24
  7.3 9.6 %collective-permute-start.1 = (f32[5,32,256]{2,1,0:T(8,128)S(1)}, f32[5,32,256]{2,1,0:T(8,128)S(1)}, u32[]{:S(2)}, u32[]{:S(2)}) collective-permute-start(f32[5,32,256]{2,1,0:T(8,128)S(1)} %get-tuple-element.17), channel_id=1, source_target_pairs={{0,2},{1,3},{2,0},{3,1},{4,6},{5,7},{6,4},{7,5},{8,10},{9,11},{10,... | collective-permute-start | bytes 491528 | tf_op jit(solution)/shard_map/ppermute | solution.py:24
  9.8 7.2 %collective-permute-start.2 = (f32[5,32,256]{2,1,0:T(8,128)S(1)}, f32[5,32,256]{2,1,0:T(8,128)S(1)}, u32[]{:S(2)}, u32[]{:S(2)}) collective-permute-start(f32[5,32,256]{2,1,0:T(8,128)S(1)} %get-tuple-element.18), channel_id=1, source_target_pairs={{0,3},{1,0},{2,1},{3,2},{4,7},{5,4},{6,5},{7,6},{8,11},{9,8},{10,9... | collective-permute-start | bytes 491528 | tf_op jit(solution)/shard_map/ppermute | solution.py:24
  17.6 17.5 %collective-permute-start.3 = (bf16[2,32,256]{2,1,0:T(8,128)(2,1)S(1)}, bf16[2,32,256]{2,1,0:T(8,128)(2,1)S(1)}, u32[]{:S(2)}, u32[]{:S(2)}) collective-permute-start(bf16[2,32,256]{2,1,0:T(8,128)(2,1)S(1)} %get-tuple-element.19), channel_id=1, source_target_pairs={{0,4},{4,8},{8,12},{12,16},{16,20},{20,24},{24,28},{28,32},{32,36}... | collective-permute-start | bytes 98312 | tf_op jit(solution)/shard_map/ppermute | solution.py:24
  20.4 14.7 %collective-permute-start.4 = (bf16[2,32,256]{2,1,0:T(8,128)(2,1)S(1)}, bf16[2,32,256]{2,1,0:T(8,128)(2,1)S(1)}, u32[]{:S(2)}, u32[]{:S(2)}) collective-permute-start(bf16[2,32,256]{2,1,0:T(8,128)(2,1)S(1)} %get-tuple-element.20), channel_id=1, source_target_pairs={{0,252},{4,0},{8,4},{12,8},{16,12},{20,16},{24,20},{28,24},{32,28}... | collective-permute-start | bytes 98312 | tf_op jit(solution)/shard_map/ppermute | solution.py:24
  20.4 14.7 %collective-permute-start.5 = (bf16[2,32,256]{2,1,0:T(8,128)(2,1)S(1)}, bf16[2,32,256]{2,1,0:T(8,128)(2,1)S(1)}, u32[]{:S(2)}, u32[]{:S(2)}) collective-permute-start(bf16[2,32,256]{2,1,0:T(8,128)(2,1)S(1)} %get-tuple-element.21), channel_id=1, source_target_pairs={{0,248},{4,252},{8,0},{12,4},{16,8},{20,12},{24,16},{28,20},{32,24... | collective-permute-start | bytes 98312 | tf_op jit(solution)/shard_map/ppermute | solution.py:24
  27.3 6.9 %collective-permute-start.6 = (bf16[1,32,256]{2,1,0:T(8,128)(2,1)S(1)}, bf16[1,32,256]{2,1,0:T(8,128)(2,1)S(1)}, u32[]{:S(2)}, u32[]{:S(2)}) collective-permute-start(bf16[1,32,256]{2,1,0:T(8,128)(2,1)S(1)} %get-tuple-element.22), channel_id=1, source_target_pairs={{0,8},{4,12},{8,16},{12,20},{16,24},{20,28},{24,32},{28,36},{32,40... | collective-permute-start | bytes 49160 | tf_op jit(solution)/shard_map/ppermute | solution.py:24
  27.3 7.8 %collective-permute-start.7 = (bf16[1,32,256]{2,1,0:T(8,128)(2,1)S(1)}, bf16[1,32,256]{2,1,0:T(8,128)(2,1)S(1)}, u32[]{:S(2)}, u32[]{:S(2)}) collective-permute-start(bf16[1,32,256]{2,1,0:T(8,128)(2,1)S(1)} %get-tuple-element.23), channel_id=1, source_target_pairs={{0,244},{4,248},{8,252},{12,0},{16,4},{20,8},{24,12},{28,16},{32,2... | collective-permute-start | bytes 49160 | tf_op jit(solution)/shard_map/ppermute | solution.py:24
  35.1 4.2 %collective-permute-start.10 = (bf16[2,4,32,256]{3,2,1,0:T(8,128)(2,1)S(1)}, bf16[2,4,32,256]{3,2,1,0:T(8,128)(2,1)S(1)}, u32[]{:S(2)}, u32[]{:S(2)}) collective-permute-start(bf16[2,4,32,256]{3,2,1,0:T(8,128)(2,1)S(1)} %shard_map.57.x0), channel_id=1, source_target_pairs={{0,3},{1,0},{2,1},{3,2},{4,7},{5,4},{6,5},{7,6},{8,11},{9,8},{10,9... | collective-permute-start | bytes 393224 | tf_op jit(solution)/shard_map/ppermute | solution.py:24
  37.2 5.4 %collective-permute-start.9 = (bf16[2,4,32,256]{3,2,1,0:T(8,128)(2,1)S(1)}, bf16[2,4,32,256]{3,2,1,0:T(8,128)(2,1)S(1)}, u32[]{:S(2)}, u32[]{:S(2)}) collective-permute-start(bf16[2,4,32,256]{3,2,1,0:T(8,128)(2,1)S(1)} %shard_map.57.x0), channel_id=1, source_target_pairs={{0,2},{1,3},{2,0},{3,1},{4,6},{5,7},{6,4},{7,5},{8,10},{9,11},{10,... | collective-permute-start | bytes 393224 | tf_op jit(solution)/shard_map/ppermute | solution.py:24
  38.0 7.9 %collective-permute-start.8 = (bf16[2,4,32,256]{3,2,1,0:T(8,128)(2,1)S(1)}, bf16[2,4,32,256]{3,2,1,0:T(8,128)(2,1)S(1)}, u32[]{:S(2)}, u32[]{:S(2)}) collective-permute-start(bf16[2,4,32,256]{3,2,1,0:T(8,128)(2,1)S(1)} %shard_map.57.x0), channel_id=1, source_target_pairs={{0,1},{1,2},{2,3},{3,0},{4,5},{5,6},{6,7},{7,4},{8,9},{9,10},{10,1... | collective-permute-start | bytes 393224 | tf_op jit(solution)/shard_map/ppermute | solution.py:24

commit v3 on v2

--- a/solution.py
+++ b/solution.py
@@ -14,8 +14,9 @@
 bf16 = jnp.bfloat16
 VM = pl.BlockSpec(memory_space=pltpu.VMEM)
 SM = pl.BlockSpec(memory_space=pltpu.SMEM)
-ANY = pl.BlockSpec(memory_space=pl.ANY)
-PARAMS = pltpu.CompilerParams(vmem_limit_bytes=40 << 20)
+ANY = pl.BlockSpec(memory_space=pltpu.HBM)
+PARAMS = pltpu.CompilerParams(vmem_limit_bytes=24 << 20)
+WIDE = pltpu.CompilerParams(vmem_limit_bytes=54300 << 10)
 ROUTES = (1, -1, -2, 2, -3)
 
 
@@ -66,7 +67,7 @@
             pltpu.VMEM((samples, rank), bf16),
             pltpu.SemaphoreType.DMA((QUARTERS + 1,)),
         ],
-        compiler_params=PARAMS,
+        compiler_params=WIDE,
     )(traces, sketch)
 
 
@@ -138,41 +139,45 @@
     lane = lax.broadcasted_iota(jnp.int32, (B, 128), 1)
     row = lax.broadcasted_iota(jnp.int32, (B, 128), 0)
     t1 = ((lane % B) == row).astype(f32)
-    half = jnp.where(lane < B, 0, B)
     groups = B // 8
     r0 = [t0[8 * i : 8 * i + 8] for i in range(groups)]
     r1 = [t1[8 * i : 8 * i + 8] for i in range(groups)]
-    h8, row8 = half[:8], row[:8]
+    half, row8 = jnp.where(lane < B, 0, B)[:8], row[:8]
+
+    def column(block, c):
+        return jnp.take_along_axis(block, half + c, axis=1, mode="promise_in_bounds")
+
     done = []
+    ahead = [[column(r0[0], j)] for j in range(8)]
     for g in range(groups):
         n = groups - g
-        cols = [
-            [
-                jnp.take_along_axis(r0[g + i], h8 + (8 * g + j), axis=1, mode="promise_in_bounds")
-                for i in range(n)
-            ]
-            for j in range(8)
+        cur = [
+            [ahead[j][-1]] + [column(r0[g + i], 8 * g + j) for i in range(1, n)] for j in range(8)
         ]
+        ahead = []
+        if n > 1:
+            ahead = [[column(r0[g + i], 8 * g + 8 + j) for i in range(2)] for j in range(8)]
         for j in range(0, 8, 2):
-            cj, ck = cols[j], cols[j + 1]
+            cj, ck = cur[j], cur[j + 1]
             a, b, d = cj[0][j : j + 1], cj[0][j + 1 : j + 2], ck[0][j + 1 : j + 2]
-            inv = 1.0 / (a * d - b * b)
-            i00, i01, i11 = d * inv, -b * inv, a * inv
-            m0 = [x * i00 + y * i01 for x, y in zip(cj, ck)]
-            m1 = [x * i01 + y * i11 for x, y in zip(cj, ck)]
-            keep = row8 > j + 1
-            m0[0] = jnp.where(keep, m0[0], 0.0)
-            m1[0] = jnp.where(keep, m1[0], 0.0)
+            det = a * d - b * b
+            inv = pl.reciprocal(det, approx=True)
+            inv = inv * (2.0 - det * inv)
+            m0 = [x * d - y * b for x, y in zip(cj, ck)]
+            m1 = [y * a - x * b for x, y in zip(cj, ck)]
+            m0[0] = jnp.where(row8 > j + 1, m0[0], 0.0)
+            m1[0] = jnp.where(row8 > j + 1, m1[0], 0.0)
+
+            def swept(top, blocks):
+                p, q = top[j : j + 1] * inv, top[j + 1 : j + 2] * inv
+                return [c - (x * p + y * q) for c, x, y in zip(blocks, m0, m1)]
+
             for k in range(j + 2, 8):
-                p, q = cols[k][0][j : j + 1], cols[k][0][j + 1 : j + 2]
-                cols[k] = [c - (x * p + y * q) for c, x, y in zip(cols[k], m0, m1)]
-            p0, q0 = r0[g][j : j + 1], r0[g][j + 1 : j + 2]
-            p1, q1 = r1[g][j : j + 1], r1[g][j + 1 : j + 2]
-            done.append((a, b, d, p1, q1))
-            for i in range(n):
-                if i > 0 or j < 6:
-                    r0[g + i] = r0[g + i] - (m0[i] * p0 + m1[i] * q0)
-                r1[g + i] = r1[g + i] - (m0[i] * p1 + m1[i] * q1)
+                cur[k] = swept(cur[k][0], cur[k])
+            ahead = [swept(c[0], c) for c in ahead]
+            done.append((a, b, d, r1[g][j : j + 1], r1[g][j + 1 : j + 2]))
+            r0[g:] = swept(r0[g], r0[g:])
+            r1[g:] = swept(r1[g], r1[g:])
     rows = []
     for a, b, d, p1, q1 in done:
         l10 = b * (1.0 / a)
@@ -181,7 +186,7 @@
     return jnp.concatenate(rows, axis=0)
 
 
-def solve_kernel(owner, x0, x1, x2, x3, o_ref, x_ref, s_ref):
+def solve_kernel(owner, x0, x1, x2, x3, o_hbm, x_ref, o_ref, sem):
     me = lax.axis_index("mesh")
     s = lax.axis_index("samp")
     ports = owner.shape[0]
@@ -195,29 +200,33 @@
     row = lax.broadcasted_iota(jnp.int32, (n, n), 0)
     col = lax.broadcasted_iota(jnp.int32, (n, n), 1)
     eye = (row == col).astype(f32)
+    blocks = []
     for p in range(2):
         for k, x in enumerate((x0, x1, x2, x3)):
             x_ref[p, k * each : (k + 1) * each] = x[p].reshape(each, n)
         x = x_ref[p]
         g = mm(x, x, ((0,), (0,)), None)
-        s_ref[p] = g + (0.1 * jnp.sum(g * eye) / n + 1e-6) * eye
+        g = g + (0.1 * jnp.sum(g * eye) / n + 1e-6) * eye
+        blocks.append([g[k * B : (k + 1) * B] for k in range(n // B)])
+    col, row = col[:B], row[:B]
     for k in range(n // B):
         lo, hi = k * B, (k + 1) * B
-        t = panel(jnp.concatenate([s_ref[0, lo:hi, lo:hi], s_ref[1, lo:hi, lo:hi]], axis=1))
+        inside = (col >= lo) & (col < hi)
+        t = panel(jnp.concatenate([s[k][:, lo:hi] for s in blocks], axis=1))
+        ys = []
         for p in range(2):
             w = t[:, p * B : (p + 1) * B]
-            c = col[:B]
-            inside = (c >= lo) & (c < hi)
-            sk = jnp.where(inside, (c - lo == row[:B]).astype(f32), s_ref[p, lo:hi, :])
-            y = mm(w, sk)
-            if hi < n:
-                u = mm(s_ref[p, hi:, lo:hi], w, ((1,), (1,)))
-                c = col[hi:]
-                old = jnp.where((c >= lo) & (c < hi), 0.0, s_ref[p, hi:, :])
-                s_ref[p, hi:, :] = old - mm(u, y)
-            s_ref[p, lo:hi, :] = y
+            sk = jnp.where(inside, (col - lo == row).astype(f32), blocks[p][k])
+            blocks[p][k] = mm(w, sk)
+            ys.append(w)
+        for i in range(k + 1, n // B):
+            for p in range(2):
+                u = mm(blocks[p][i][:, lo:hi], ys[p], ((1,), (1,)))
+                blocks[p][i] = jnp.where(inside, 0.0, blocks[p][i]) - mm(u, blocks[p][k])
+    stores = []
     for p in range(2):
-        w = jnp.where(col <= row, s_ref[p], 0.0)
+        w = [jnp.where(col <= row + k * B, s, 0.0) for k, s in enumerate(blocks[p])]
+        w = jnp.concatenate(w, axis=0)
         w0 = w.astype(bf16)
         e = w - w0.astype(f32)
         w1 = e.astype(bf16)
@@ -229,7 +238,12 @@
             q = lax.rem(s - k + QUARTERS, QUARTERS)
             for j in range(FACES):
                 at = pl.multiple_of(j * QUARTERS * rows + q * rows, rows)
-                o_ref[slots[p], pl.ds(at, rows), :] = y[k * each + j * rows : k * each + (j + 1) * rows]
+                o_ref[p, pl.ds(at, rows), :] = y[k * each + j * rows : k * each + (j + 1) * rows]
+        store = pltpu.make_async_copy(o_ref.at[p], o_hbm.at[slots[p]], sem.at[p])
+        store.start()
+        stores.append(store)
+    for store in stores:
+        store.wait()
 
 
 def solve(port_owner, pieces):
@@ -239,8 +253,12 @@
         solve_kernel,
         out_shape=jax.ShapeDtypeStruct((2, height, n), f32),
         in_specs=[SM] + [VM] * QUARTERS,
-        out_specs=VM,
-        scratch_shapes=[pltpu.VMEM((2, height, n), bf16), pltpu.VMEM((2, n, n), f32)],
+        out_specs=ANY,
+        scratch_shapes=[
+            pltpu.VMEM((2, height, n), bf16),
+            pltpu.VMEM((2, height, n), f32),
+            pltpu.SemaphoreType.DMA((2,)),
+        ],
         compiler_params=PARAMS,
     )(port_owner, *pieces)
 

time: 58.1 us -> 54.3 us (0.935)
  local copies, waits for them, and re-layouts: 2.97 us -> 0.01 us
  Pallas kernels: 15 us -> 14 us
    unnamed x8 -> x4, local copies, waits for them, and re-layouts: 2.97 us -> 0.01 us
    pallas_call x1, Pallas kernels: 12 us -> 9.9 us  [solve(): pl.pallas_call(solve_kernel, out_shape=jax.ShapeDtypeStruct((2, height, n...]
    pallas_call x1, Pallas kernels: 2.25 us -> 3.42 us  [sketch_parts(): pl.pallas_call(sketch_kernel, out_shape=[part] * QUARTERS, in_specs=[ANY,...]
where the time goes in v3:
time: 54.3 us; the launch traced here: 54.2 us
  starting transfers between devices  25.6 us (47%)
  Pallas kernels  14 us (26%)
  waiting for transfers between devices  13.7 us (25%)
  between operations  0.86 us (2%)
    ppermute x11, starting transfers between devices, shifted(): lax.ppermute(block, axis, [(i, (i + distance) % n) for i in range(n)])  25.6 us
    ppermute x11, waiting for transfers between devices, shifted(): lax.ppermute(block, axis, [(i, (i + distance) % n) for i in range(n)])  13.7 us
    pallas_call x1, Pallas kernels, solve(): pl.pallas_call(solve_kernel, out_shape=jax.ShapeDtypeStruct((2, height, n...  9.9 us
    pallas_call x1, Pallas kernels, sketch_parts(): pl.pallas_call(sketch_kernel, out_shape=[part] * QUARTERS, in_specs=[ANY,...  3.42 us
  transfers between devices with their start and end apart: 11, of which 5 were waited for; matrix products, arithmetic and copies ran while one was open for 0% of the time, Pallas kernels for 0%

profile of v3, /device:TPU:1, one launch (start us, length us, event | category | flops | bytes accessed | tf_op | source)
XLA Modules:
  0.0 54.2 jit_solution(1657780274661576294)
XLA Ops:
  0.0 0.0 copy-start
  0.0 0.0 copy-start.1
  0.0 3.4 %shard_map.55 = (f32[5,32,256]{2,1,0:T(8,128)S(1)}, f32[5,32,256]{2,1,0:T(8,128)S(1)}, f32[5,32,256]{2,1,0:T(8,128)S(1)}, f32[5,32,256]{2,1,0:T(8,128)S(1)}) custom-call(bf16[5,128,2048]{2,1,0:T(8,128)(2,1)} %t_hbm.1, bf16[2048,256]{1,0:T(8,128)(2,1)} %r_hbm.1), custom_call_target="tpu_custom_call" | custom-call | tf_op jit(solution)/shard_map/pallas_call | solution.py:60
  3.4 2.1 %collective-permute-start = (f32[5,32,256]{2,1,0:T(8,128)S(1)}, f32[5,32,256]{2,1,0:T(8,128)S(1)}, u32[]{:S(2)}, u32[]{:S(2)}) collective-permute-start(f32[5,32,256]{2,1,0:T(8,128)S(1)} %get-tuple-element.16), channel_id=1, source_target_pairs={{0,1},{1,2},{2,3},{3,0},{4,5},{5,6},{6,7},{7,4},{8,9},{9,10},{10,1... | collective-permute-start | bytes 491528 | tf_op jit(solution)/shard_map/ppermute | solution.py:25
  5.5 2.4 %collective-permute-start.1 = (f32[5,32,256]{2,1,0:T(8,128)S(1)}, f32[5,32,256]{2,1,0:T(8,128)S(1)}, u32[]{:S(2)}, u32[]{:S(2)}) collective-permute-start(f32[5,32,256]{2,1,0:T(8,128)S(1)} %get-tuple-element.17), channel_id=1, source_target_pairs={{0,2},{1,3},{2,0},{3,1},{4,6},{5,7},{6,4},{7,5},{8,10},{9,11},{10,... | collective-permute-start | bytes 491528 | tf_op jit(solution)/shard_map/ppermute | solution.py:25
  8.0 1.2 %collective-permute-start.2 = (f32[5,32,256]{2,1,0:T(8,128)S(1)}, f32[5,32,256]{2,1,0:T(8,128)S(1)}, u32[]{:S(2)}, u32[]{:S(2)}) collective-permute-start(f32[5,32,256]{2,1,0:T(8,128)S(1)} %get-tuple-element.18), channel_id=1, source_target_pairs={{0,3},{1,0},{2,1},{3,2},{4,7},{5,4},{6,5},{7,6},{8,11},{9,8},{10,9... | collective-permute-start | bytes 491528 | tf_op jit(solution)/shard_map/ppermute | solution.py:25
  9.8 0.0 collective-permute-done.b
  9.8 5.3 %collective-permute-done.1.c = f32[5,32,256]{2,1,0:T(8,128)S(1)} collective-permute-done((f32[5,32,256]{2,1,0:T(8,128)S(1)}, f32[5,32,256]{2,1,0:T(8,128)S(1)}, u32[]{:S(2)}, u32[]{:S(2)}) %collective-permute-start.1) | collective-permute-done | bytes 163872 | tf_op jit(solution)/shard_map/ppermute | solution.py:25
  15.2 0.0 collective-permute-done.2.d
  15.2 0.0 copy-done
  15.2 0.0 copy-done.1
  15.2 0.6 %shard_map.56 = (bf16[2,32,256]{2,1,0:T(8,128)(2,1)S(1)}, bf16[2,32,256]{2,1,0:T(8,128)(2,1)S(1)}, bf16[2,32,256]{2,1,0:T(8,128)(2,1)S(1)}, bf16[1,32,256]{2,1,0...) custom-call(s32[5]{0:T(128)S(1)} %copy-done.1, s32[1]{0:T(128)S(6)} %copy.6.count, ...), custom_call_target="tpu_custom_call" | custom-call | tf_op jit(solution)/shard_map/pallas_call | solution.py:103
  15.8 2.8 %collective-permute-start.3 = (bf16[2,32,256]{2,1,0:T(8,128)(2,1)S(1)}, bf16[2,32,256]{2,1,0:T(8,128)(2,1)S(1)}, u32[]{:S(2)}, u32[]{:S(2)}) collective-permute-start(bf16[2,32,256]{2,1,0:T(8,128)(2,1)S(1)} %get-tuple-element.19), channel_id=1, source_target_pairs={{0,4},{4,8},{8,12},{12,16},{16,20},{20,24},{24,28},{28,32},{32,36}... | collective-permute-start | bytes 98312 | tf_op jit(solution)/shard_map/ppermute | solution.py:25
  18.6 0.0 collective-permute-start.4
  18.6 6.9 %collective-permute-start.5 = (bf16[2,32,256]{2,1,0:T(8,128)(2,1)S(1)}, bf16[2,32,256]{2,1,0:T(8,128)(2,1)S(1)}, u32[]{:S(2)}, u32[]{:S(2)}) collective-permute-start(bf16[2,32,256]{2,1,0:T(8,128)(2,1)S(1)} %get-tuple-element.21), channel_id=1, source_target_pairs={{0,248},{4,252},{8,0},{12,4},{16,8},{20,12},{24,16},{28,20},{32,24... | collective-permute-start | bytes 98312 | tf_op jit(solution)/shard_map/ppermute | solution.py:25
  25.5 0.0 collective-permute-start.6
  25.5 6.9 %collective-permute-start.7 = (bf16[1,32,256]{2,1,0:T(8,128)(2,1)S(1)}, bf16[1,32,256]{2,1,0:T(8,128)(2,1)S(1)}, u32[]{:S(2)}, u32[]{:S(2)}) collective-permute-start(bf16[1,32,256]{2,1,0:T(8,128)(2,1)S(1)} %get-tuple-element.23), channel_id=1, source_target_pairs={{0,244},{4,248},{8,252},{12,0},{16,4},{20,8},{24,12},{28,16},{32,2... | collective-permute-start | bytes 49160 | tf_op jit(solution)/shard_map/ppermute | solution.py:25
  32.4 0.0 collective-permute-done.6.p2
  32.4 0.9 %collective-permute-done.7.m3 = bf16[1,32,256]{2,1,0:T(8,128)(2,1)S(1)} collective-permute-done((bf16[1,32,256]{2,1,0:T(8,128)(2,1)S(1)}, bf16[1,32,256]{2,1,0:T(8,128)(2,1)S(1)}, u32[]{:S(2)}, u32[]{:S(2)}) %collective-permute-start.7) | collective-permute-done | bytes 16416 | tf_op jit(solution)/shard_map/ppermute | solution.py:25
  33.3 0.0 collective-permute-done.3.p1
  33.3 0.0 collective-permute-done.4.m1
  33.3 0.0 collective-permute-done.5.m2
  33.3 0.1 shard_map.57.x0
  33.3 2.1 %collective-permute-start.10 = (bf16[2,4,32,256]{3,2,1,0:T(8,128)(2,1)S(1)}, bf16[2,4,32,256]{3,2,1,0:T(8,128)(2,1)S(1)}, u32[]{:S(2)}, u32[]{:S(2)}) collective-permute-start(bf16[2,4,32,256]{3,2,1,0:T(8,128)(2,1)S(1)} %shard_map.57.x0), channel_id=1, source_target_pairs={{0,3},{1,0},{2,1},{3,2},{4,7},{5,4},{6,5},{7,6},{8,11},{9,8},{10,9... | collective-permute-start | bytes 393224 | tf_op jit(solution)/shard_map/ppermute | solution.py:25
  35.4 0.9 %collective-permute-start.9 = (bf16[2,4,32,256]{3,2,1,0:T(8,128)(2,1)S(1)}, bf16[2,4,32,256]{3,2,1,0:T(8,128)(2,1)S(1)}, u32[]{:S(2)}, u32[]{:S(2)}) collective-permute-start(bf16[2,4,32,256]{3,2,1,0:T(8,128)(2,1)S(1)} %shard_map.57.x0), channel_id=1, source_target_pairs={{0,2},{1,3},{2,0},{3,1},{4,6},{5,7},{6,4},{7,5},{8,10},{9,11},{10,... | collective-permute-start | bytes 393224 | tf_op jit(solution)/shard_map/ppermute | solution.py:25
  36.2 0.4 collective-permute-start.8
  36.6 0.9 %collective-permute-done.10.x3 = bf16[2,4,32,256]{3,2,1,0:T(8,128)(2,1)S(1)} collective-permute-done((bf16[2,4,32,256]{3,2,1,0:T(8,128)(2,1)S(1)}, bf16[2,4,32,256]{3,2,1,0:T(8,128)(2,1)S(1)}, u32[]{:S(2)}, u32[]{:S(2)}) %collective-permute-start.10) | collective-permute-done | bytes 131104 | tf_op jit(solution)/shard_map/ppermute | solution.py:25
  37.6 3.2 %collective-permute-done.9.x2 = bf16[2,4,32,256]{3,2,1,0:T(8,128)(2,1)S(1)} collective-permute-done((bf16[2,4,32,256]{3,2,1,0:T(8,128)(2,1)S(1)}, bf16[2,4,32,256]{3,2,1,0:T(8,128)(2,1)S(1)}, u32[]{:S(2)}, u32[]{:S(2)}) %collective-permute-start.9) | collective-permute-done | bytes 131104 | tf_op jit(solution)/shard_map/ppermute | solution.py:25
  40.8 3.3 %collective-permute-done.8.x1 = bf16[2,4,32,256]{3,2,1,0:T(8,128)(2,1)S(1)} collective-permute-done((bf16[2,4,32,256]{3,2,1,0:T(8,128)(2,1)S(1)}, bf16[2,4,32,256]{3,2,1,0:T(8,128)(2,1)S(1)}, u32[]{:S(2)}, u32[]{:S(2)}) %collective-permute-start.8) | collective-permute-done | bytes 131104 | tf_op jit(solution)/shard_map/ppermute | solution.py:25
  44.1 9.9 %shard_map.58 = f32[2,512,256]{2,1,0:T(8,128)} custom-call(s32[64]{0:T(128)S(1)} %copy-done, bf16[2,4,32,256]{3,2,1,0:T(8,128)(2,1)S(1)} %shard_map.57.x0, bf16[2,4,32,256]{3,2,1,0:T(8,128)(2,1)S(1)} %collective-permute-done.8.x1, bf16[2,4,32,256]{3,2,1,0:T(8,128)(2,1)S(1)} %collective-permute-done.9.x2, bf16[2,4,32,256]{3,2,1,0:T(8,128)(2,1)S(1)} %collective-permute-done.10.x3), custom_call_target="tpu_custom_call" | custom-call | tf_op jit(solution)/shard_map/pallas_call | solution.py:252
Async XLA Ops:
  0.0 15.2 %copy-start = (s32[64]{0:T(128)S(1)}, s32[64]{0:T(128)}, u32[]{:S(2)}) copy-start(s32[64]{0:T(128)} %owner.3) | copy-start | bytes 772
  0.0 15.2 %copy-start.1 = (s32[5]{0:T(128)S(1)}, s32[5]{0:T(128)}, u32[]{:S(2)}) copy-start(s32[5]{0:T(128)} %port.1) | copy-start | bytes 64
  3.4 6.4 %collective-permute-start = (f32[5,32,256]{2,1,0:T(8,128)S(1)}, f32[5,32,256]{2,1,0:T(8,128)S(1)}, u32[]{:S(2)}, u32[]{:S(2)}) collective-permute-start(f32[5,32,256]{2,1,0:T(8,128)S(1)} %get-tuple-element.16), channel_id=1, source_target_pairs={{0,1},{1,2},{2,3},{3,0},{4,5},{5,6},{6,7},{7,4},{8,9},{9,10},{10,1... | collective-permute-start | bytes 491528 | tf_op jit(solution)/shard_map/ppermute | solution.py:25
  5.5 9.6 %collective-permute-start.1 = (f32[5,32,256]{2,1,0:T(8,128)S(1)}, f32[5,32,256]{2,1,0:T(8,128)S(1)}, u32[]{:S(2)}, u32[]{:S(2)}) collective-permute-start(f32[5,32,256]{2,1,0:T(8,128)S(1)} %get-tuple-element.17), channel_id=1, source_target_pairs={{0,2},{1,3},{2,0},{3,1},{4,6},{5,7},{6,4},{7,5},{8,10},{9,11},{10,... | collective-permute-start | bytes 491528 | tf_op jit(solution)/shard_map/ppermute | solution.py:25
  8.0 7.2 %collective-permute-start.2 = (f32[5,32,256]{2,1,0:T(8,128)S(1)}, f32[5,32,256]{2,1,0:T(8,128)S(1)}, u32[]{:S(2)}, u32[]{:S(2)}) collective-permute-start(f32[5,32,256]{2,1,0:T(8,128)S(1)} %get-tuple-element.18), channel_id=1, source_target_pairs={{0,3},{1,0},{2,1},{3,2},{4,7},{5,4},{6,5},{7,6},{8,11},{9,8},{10,9... | collective-permute-start | bytes 491528 | tf_op jit(solution)/shard_map/ppermute | solution.py:25
  15.8 17.5 %collective-permute-start.3 = (bf16[2,32,256]{2,1,0:T(8,128)(2,1)S(1)}, bf16[2,32,256]{2,1,0:T(8,128)(2,1)S(1)}, u32[]{:S(2)}, u32[]{:S(2)}) collective-permute-start(bf16[2,32,256]{2,1,0:T(8,128)(2,1)S(1)} %get-tuple-element.19), channel_id=1, source_target_pairs={{0,4},{4,8},{8,12},{12,16},{16,20},{20,24},{24,28},{28,32},{32,36}... | collective-permute-start | bytes 98312 | tf_op jit(solution)/shard_map/ppermute | solution.py:25
  18.6 14.7 %collective-permute-start.4 = (bf16[2,32,256]{2,1,0:T(8,128)(2,1)S(1)}, bf16[2,32,256]{2,1,0:T(8,128)(2,1)S(1)}, u32[]{:S(2)}, u32[]{:S(2)}) collective-permute-start(bf16[2,32,256]{2,1,0:T(8,128)(2,1)S(1)} %get-tuple-element.20), channel_id=1, source_target_pairs={{0,252},{4,0},{8,4},{12,8},{16,12},{20,16},{24,20},{28,24},{32,28}... | collective-permute-start | bytes 98312 | tf_op jit(solution)/shard_map/ppermute | solution.py:25
  18.6 14.7 %collective-permute-start.5 = (bf16[2,32,256]{2,1,0:T(8,128)(2,1)S(1)}, bf16[2,32,256]{2,1,0:T(8,128)(2,1)S(1)}, u32[]{:S(2)}, u32[]{:S(2)}) collective-permute-start(bf16[2,32,256]{2,1,0:T(8,128)(2,1)S(1)} %get-tuple-element.21), channel_id=1, source_target_pairs={{0,248},{4,252},{8,0},{12,4},{16,8},{20,12},{24,16},{28,20},{32,24... | collective-permute-start | bytes 98312 | tf_op jit(solution)/shard_map/ppermute | solution.py:25
  25.5 6.9 %collective-permute-start.6 = (bf16[1,32,256]{2,1,0:T(8,128)(2,1)S(1)}, bf16[1,32,256]{2,1,0:T(8,128)(2,1)S(1)}, u32[]{:S(2)}, u32[]{:S(2)}) collective-permute-start(bf16[1,32,256]{2,1,0:T(8,128)(2,1)S(1)} %get-tuple-element.22), channel_id=1, source_target_pairs={{0,8},{4,12},{8,16},{12,20},{16,24},{20,28},{24,32},{28,36},{32,40... | collective-permute-start | bytes 49160 | tf_op jit(solution)/shard_map/ppermute | solution.py:25
  25.5 7.8 %collective-permute-start.7 = (bf16[1,32,256]{2,1,0:T(8,128)(2,1)S(1)}, bf16[1,32,256]{2,1,0:T(8,128)(2,1)S(1)}, u32[]{:S(2)}, u32[]{:S(2)}) collective-permute-start(bf16[1,32,256]{2,1,0:T(8,128)(2,1)S(1)} %get-tuple-element.23), channel_id=1, source_target_pairs={{0,244},{4,248},{8,252},{12,0},{16,4},{20,8},{24,12},{28,16},{32,2... | collective-permute-start | bytes 49160 | tf_op jit(solution)/shard_map/ppermute | solution.py:25
  33.3 4.3 %collective-permute-start.10 = (bf16[2,4,32,256]{3,2,1,0:T(8,128)(2,1)S(1)}, bf16[2,4,32,256]{3,2,1,0:T(8,128)(2,1)S(1)}, u32[]{:S(2)}, u32[]{:S(2)}) collective-permute-start(bf16[2,4,32,256]{3,2,1,0:T(8,128)(2,1)S(1)} %shard_map.57.x0), channel_id=1, source_target_pairs={{0,3},{1,0},{2,1},{3,2},{4,7},{5,4},{6,5},{7,6},{8,11},{9,8},{10,9... | collective-permute-start | bytes 393224 | tf_op jit(solution)/shard_map/ppermute | solution.py:25
  35.4 5.4 %collective-permute-start.9 = (bf16[2,4,32,256]{3,2,1,0:T(8,128)(2,1)S(1)}, bf16[2,4,32,256]{3,2,1,0:T(8,128)(2,1)S(1)}, u32[]{:S(2)}, u32[]{:S(2)}) collective-permute-start(bf16[2,4,32,256]{3,2,1,0:T(8,128)(2,1)S(1)} %shard_map.57.x0), channel_id=1, source_target_pairs={{0,2},{1,3},{2,0},{3,1},{4,6},{5,7},{6,4},{7,5},{8,10},{9,11},{10,... | collective-permute-start | bytes 393224 | tf_op jit(solution)/shard_map/ppermute | solution.py:25
  36.2 7.9 %collective-permute-start.8 = (bf16[2,4,32,256]{3,2,1,0:T(8,128)(2,1)S(1)}, bf16[2,4,32,256]{3,2,1,0:T(8,128)(2,1)S(1)}, u32[]{:S(2)}, u32[]{:S(2)}) collective-permute-start(bf16[2,4,32,256]{3,2,1,0:T(8,128)(2,1)S(1)} %shard_map.57.x0), channel_id=1, source_target_pairs={{0,1},{1,2},{2,3},{3,0},{4,5},{5,6},{6,7},{7,4},{8,9},{9,10},{10,1... | collective-permute-start | bytes 393224 | tf_op jit(solution)/shard_map/ppermute | solution.py:25

commit v4 on v3

--- a/solution.py
+++ b/solution.py
@@ -1,3 +1,5 @@
+import functools
+
 import jax
 import jax.numpy as jnp
 from jax import lax
@@ -17,7 +19,8 @@
 ANY = pl.BlockSpec(memory_space=pltpu.HBM)
 PARAMS = pltpu.CompilerParams(vmem_limit_bytes=24 << 20)
 WIDE = pltpu.CompilerParams(vmem_limit_bytes=54300 << 10)
-ROUTES = (1, -1, -2, 2, -3)
+TURNS = (0, 2, 1, 3)
+ROUTES = (2, -2, -3, 1, -1)
 
 
 def shifted(block, axis, distance):
@@ -29,49 +32,47 @@
     return lax.dot_general(a, b, (dims, ((), ())), precision=prec, preferred_element_type=f32)
 
 
-def sketch_kernel(t_hbm, r_hbm, o0, o1, o2, o3, t, r, sem):
+def sketch_kernel(turns, t_hbm, r_hbm, *refs):
+    outs, (t, r, sem) = refs[: len(turns)], refs[len(turns) :]
     s = lax.axis_index("samp")
-    outs = (o0, o1, o2, o3)
-    slots, rows = o0.shape[0], o0.shape[1]
-    order = (2, 1, 3, 0)
-    load_r = pltpu.make_async_copy(r_hbm, r, sem.at[4])
+    slots, rows = outs[0].shape[:2]
+    load_r = pltpu.make_async_copy(r_hbm, r, sem.at[len(turns)])
     load_r.start()
     loads = []
-    for k in order:
+    for i, k in enumerate(turns):
         c = lax.rem(s + k, QUARTERS)
         load = pltpu.make_async_copy(
-            t_hbm.at[:, pl.ds(pl.multiple_of(c * rows, rows), rows), :], t.at[k], sem.at[k]
+            t_hbm.at[:, pl.ds(pl.multiple_of(c * rows, rows), rows), :], t.at[i], sem.at[i]
         )
         load.start()
         loads.append(load)
     load_r.wait()
-    for k, load in zip(order, loads):
+    for i, load in enumerate(loads):
         load.wait()
-        x = t[k].reshape(slots * rows, t.shape[3])
-        y = mm(x, r[...], prec=None)
-        outs[k][...] = y.reshape(outs[k].shape)
-
-
-def sketch_parts(traces, sketch):
+        y = mm(t[i].reshape(slots * rows, t.shape[3]), r[...], prec=None)
+        outs[i][...] = y.reshape(outs[i].shape)
+
+
+def sketch_parts(traces, sketch, turns):
     slots, cells, samples = traces.shape
     rows = cells // QUARTERS
     rank = sketch.shape[1]
     part = jax.ShapeDtypeStruct((slots, rows, rank), f32)
     return pl.pallas_call(
-        sketch_kernel,
-        out_shape=[part] * QUARTERS,
+        functools.partial(sketch_kernel, turns),
+        out_shape=[part] * len(turns),
         in_specs=[ANY, ANY],
-        out_specs=[VM] * QUARTERS,
+        out_specs=[VM] * len(turns),
         scratch_shapes=[
-            pltpu.VMEM((QUARTERS, slots, rows, samples), bf16),
+            pltpu.VMEM((len(turns), slots, rows, samples), bf16),
             pltpu.VMEM((samples, rank), bf16),
-            pltpu.SemaphoreType.DMA((QUARTERS + 1,)),
+            pltpu.SemaphoreType.DMA((len(turns) + 1,)),
         ],
         compiler_params=WIDE,
     )(traces, sketch)
 
 
-def place_kernel(port, count, owner, a, b, c, d, p1, m1, m2, p2, m3, here, total):
+def place_kernel(port, count, owner, a, b, c, d, p2, m2, m3, p1, m1, here, total):
     me = lax.axis_index("mesh")
     n = owner.shape[0]
     total[...] = ((a[...] + b[...]) + (c[...] + d[...])).astype(bf16)
@@ -94,15 +95,16 @@
         out[1] = tile(near + 1, 2)
     p2[0] = tile(0, 2)
     m3[0] = tile(4, 1)
+    p2[1] = p2[0]
+    m3[1] = m3[0]
 
 
 def place(face_port, tile_count, port_owner, parts):
     slots, rows, rank = parts[0].shape
     two = jax.ShapeDtypeStruct((2, rows, rank), bf16)
-    one = jax.ShapeDtypeStruct((1, rows, rank), bf16)
     return pl.pallas_call(
         place_kernel,
-        out_shape=[two, two, two, one, one, two],
+        out_shape=[two] * 6,
         in_specs=[SM] * 3 + [VM] * 4,
         out_specs=[VM] * 6,
         scratch_shapes=[pltpu.VMEM((slots, rows, rank), bf16)],
@@ -110,7 +112,7 @@
     )(face_port, tile_count, port_owner, *parts)
 
 
-def pick_kernel(p1, m1, m2, p2, m3, here, out):
+def pick_kernel(p2, m2, m3, p1, m1, here, out):
     near = [p1[0], here[0], m1[0], m2[0], m3[0]]
     far = [p2[0], p1[1], here[1], m1[1], m2[1]]
     for lean, tiles in enumerate((near, far)):
@@ -235,7 +237,7 @@
         acc = mm(x, w2, ((1,), (1,)), None) + mm(x, w1, ((1,), (1,)), None)
         y = acc + mm(x, w0, ((1,), (1,)), None)
         for k in range(QUARTERS):
-            q = lax.rem(s - k + QUARTERS, QUARTERS)
+            q = lax.rem(s - TURNS[k] + QUARTERS, QUARTERS)
             for j in range(FACES):
                 at = pl.multiple_of(j * QUARTERS * rows + q * rows, rows)
                 o_ref[p, pl.ds(at, rows), :] = y[k * each + j * rows : k * each + (j + 1) * rows]
@@ -264,14 +266,15 @@
 
 
 def body(traces, sketch, face_port, face_pos, tile_count, port_owner):
-    own, k1, k2, k3 = sketch_parts(traces, sketch)
+    (k2,) = sketch_parts(traces, sketch, (2,))
+    k1, k3, own = sketch_parts(traces, sketch, (1, 3, 0))
     k2 = shifted(k2, "samp", 2)
     k1 = shifted(k1, "samp", 1)
     k3 = shifted(k3, "samp", -1)
     *sends, here = place(face_port, tile_count, port_owner, (own, k1, k2, k3))
     tiles = [shifted(x, "mesh", distance) for x, distance in zip(sends, ROUTES)]
     mine = pick((*tiles, here))
-    pieces = [mine] + [shifted(mine, "samp", k) for k in range(1, QUARTERS)]
+    pieces = [mine] + [shifted(mine, "samp", k) for k in TURNS[1:]]
     return solve(port_owner, pieces)
 
 

time: 54.3 us -> 50.6 us (0.932)
  starting transfers between devices: 25.6 us -> 22.8 us
  waiting for transfers between devices: 13.7 us -> 11.4 us
  Pallas kernels: 14 us -> 15.1 us
    ppermute x11, starting transfers between devices: 25.6 us -> 22.8 us  [shifted(): lax.ppermute(block, axis, [(i, (i + distance) % n) for i in range(n)])]
    ppermute x11, waiting for transfers between devices: 13.7 us -> 11.4 us  [shifted(): lax.ppermute(block, axis, [(i, (i + distance) % n) for i in range(n)])]
    pallas_call x2 -> x3, Pallas kernels: 4.05 us -> 5.15 us  [the longest x2 4.51 us: sketch_parts(): pl.pallas_call(functools.partial(sketch_kernel, turns), out_shape=[part]...]
  transfers between devices with their start and end apart: 11 -> 11, of which waited for: 5 -> 6; matrix products, arithmetic and copies ran while one was open for 0% -> 0% of each run, Pallas kernels for 0% -> 5%
where the time goes in v4:
time: 50.6 us; the launch traced here: 50.2 us
  starting transfers between devices  22.8 us (45%)
  Pallas kernels  15.1 us (30%)
  waiting for transfers between devices  11.4 us (23%)
  between operations  0.88 us (2%)
    ppermute x11, starting transfers between devices, shifted(): lax.ppermute(block, axis, [(i, (i + distance) % n) for i in range(n)])  22.8 us
    ppermute x11, waiting for transfers between devices, shifted(): lax.ppermute(block, axis, [(i, (i + distance) % n) for i in range(n)])  11.4 us
    pallas_call x1, Pallas kernels, solve(): pl.pallas_call(solve_kernel, out_shape=jax.ShapeDtypeStruct((2, height, n...  9.9 us
    pallas_call x2, Pallas kernels, sketch_parts(): pl.pallas_call(functools.partial(sketch_kernel, turns), out_shape=[part]...  4.51 us
  transfers between devices with their start and end apart: 11, of which 6 were waited for; matrix products, arithmetic and copies ran while one was open for 0% of the time, Pallas kernels for 5%

profile of v4, /device:TPU:1, one launch (start us, length us, event | category | flops | bytes accessed | tf_op | source)
XLA Modules:
  0.0 50.2 jit_solution(12274376760356299635)
XLA Ops:
  0.0 1.8 %shard_map.56 = f32[5,32,256]{2,1,0:T(8,128)S(1)} custom-call(bf16[5,128,2048]{2,1,0:T(8,128)(2,1)} %t_hbm.3, bf16[2048,256]{1,0:T(8,128)(2,1)} %r_hbm.3), custom_call_target="tpu_custom_call" | custom-call | tf_op jit(solution)/shard_map/pallas_call | solution.py:61
  1.8 0.0 copy-start
  1.8 0.0 copy-start.1
  1.8 3.7 %collective-permute-start.1 = (f32[5,32,256]{2,1,0:T(8,128)S(1)}, f32[5,32,256]{2,1,0:T(8,128)S(1)}, u32[]{:S(2)}, u32[]{:S(2)}) collective-permute-start(f32[5,32,256]{2,1,0:T(8,128)S(1)} %shard_map.56), channel_id=1, source_target_pairs={{0,2},{1,3},{2,0},{3,1},{4,6},{5,7},{6,4},{7,5},{8,10},{9,11},{10,... | collective-permute-start | bytes 491528 | tf_op jit(solution)/shard_map/ppermute | solution.py:28
  5.5 2.8 %shard_map.55 = (f32[5,32,256]{2,1,0:T(8,128)S(1)}, f32[5,32,256]{2,1,0:T(8,128)S(1)}, f32[5,32,256]{2,1,0:T(8,128)S(1)}) custom-call(bf16[5,128,2048]{2,1,0:T(8,128)(2,1)} %t_hbm.3, bf16[2048,256]{1,0:T(8,128)(2,1)} %r_hbm.3), custom_call_target="tpu_custom_call" | custom-call | tf_op jit(solution)/shard_map/pallas_call | solution.py:61
  8.2 0.4 collective-permute-start
  8.6 2.4 %collective-permute-start.2 = (f32[5,32,256]{2,1,0:T(8,128)S(1)}, f32[5,32,256]{2,1,0:T(8,128)S(1)}, u32[]{:S(2)}, u32[]{:S(2)}) collective-permute-start(f32[5,32,256]{2,1,0:T(8,128)S(1)} %get-tuple-element.16), channel_id=1, source_target_pairs={{0,3},{1,0},{2,1},{3,2},{4,7},{5,4},{6,5},{7,6},{8,11},{9,8},{10,9... | collective-permute-start | bytes 491528 | tf_op jit(solution)/shard_map/ppermute | solution.py:28
  11.6 0.0 collective-permute-done.1.c
  11.6 2.6 %collective-permute-done.b = f32[5,32,256]{2,1,0:T(8,128)S(1)} collective-permute-done((f32[5,32,256]{2,1,0:T(8,128)S(1)}, f32[5,32,256]{2,1,0:T(8,128)S(1)}, u32[]{:S(2)}, u32[]{:S(2)}) %collective-permute-start) | collective-permute-done | bytes 163872 | tf_op jit(solution)/shard_map/ppermute | solution.py:28
  14.2 0.0 collective-permute-done.2.d
  14.2 0.0 copy-done
  14.3 0.0 copy-done.1
  14.3 0.6 %shard_map.57 = (bf16[2,32,256]{2,1,0:T(8,128)(2,1)S(1)}, bf16[2,32,256]{2,1,0:T(8,128)(2,1)S(1)}, bf16[2,32,256]{2,1,0:T(8,128)(2,1)S(1)}, bf16[2,32,256]{2,1,0...) custom-call(s32[5]{0:T(128)S(1)} %copy-done.1, s32[1]{0:T(128)S(6)} %copy.6.count, ...), custom_call_target="tpu_custom_call" | custom-call | tf_op jit(solution)/shard_map/pallas_call | solution.py:105
  14.9 1.4 %collective-permute-start.3 = (bf16[2,32,256]{2,1,0:T(8,128)(2,1)S(1)}, bf16[2,32,256]{2,1,0:T(8,128)(2,1)S(1)}, u32[]{:S(2)}, u32[]{:S(2)}) collective-permute-start(bf16[2,32,256]{2,1,0:T(8,128)(2,1)S(1)} %get-tuple-element.17), channel_id=1, source_target_pairs={{0,8},{4,12},{8,16},{12,20},{16,24},{20,28},{24,32},{28,36},{32,40... | collective-permute-start | bytes 98312 | tf_op jit(solution)/shard_map/ppermute | solution.py:28
  16.3 6.8 %collective-permute-start.4 = (bf16[2,32,256]{2,1,0:T(8,128)(2,1)S(1)}, bf16[2,32,256]{2,1,0:T(8,128)(2,1)S(1)}, u32[]{:S(2)}, u32[]{:S(2)}) collective-permute-start(bf16[2,32,256]{2,1,0:T(8,128)(2,1)S(1)} %get-tuple-element.18), channel_id=1, source_target_pairs={{0,248},{4,252},{8,0},{12,4},{16,8},{20,12},{24,16},{28,20},{32,24... | collective-permute-start | bytes 98312 | tf_op jit(solution)/shard_map/ppermute | solution.py:28
  23.1 3.7 %collective-permute-start.5 = (bf16[2,32,256]{2,1,0:T(8,128)(2,1)S(1)}, bf16[2,32,256]{2,1,0:T(8,128)(2,1)S(1)}, u32[]{:S(2)}, u32[]{:S(2)}) collective-permute-start(bf16[2,32,256]{2,1,0:T(8,128)(2,1)S(1)} %get-tuple-element.19), channel_id=1, source_target_pairs={{0,244},{4,248},{8,252},{12,0},{16,4},{20,8},{24,12},{28,16},{32,2... | collective-permute-start | bytes 98312 | tf_op jit(solution)/shard_map/ppermute | solution.py:28
  26.8 0.0 collective-permute-start.6
  26.8 0.5 %collective-permute-start.7 = (bf16[2,32,256]{2,1,0:T(8,128)(2,1)S(1)}, bf16[2,32,256]{2,1,0:T(8,128)(2,1)S(1)}, u32[]{:S(2)}, u32[]{:S(2)}) collective-permute-start(bf16[2,32,256]{2,1,0:T(8,128)(2,1)S(1)} %get-tuple-element.21), channel_id=1, source_target_pairs={{0,252},{4,0},{8,4},{12,8},{16,12},{20,16},{24,20},{28,24},{32,28}... | collective-permute-start | bytes 98312 | tf_op jit(solution)/shard_map/ppermute | solution.py:28
  27.3 0.0 collective-permute-done.3.p2
  27.3 0.0 collective-permute-done.4.m2
  27.3 0.6 %collective-permute-done.5.m3 = bf16[2,32,256]{2,1,0:T(8,128)(2,1)S(1)} collective-permute-done((bf16[2,32,256]{2,1,0:T(8,128)(2,1)S(1)}, bf16[2,32,256]{2,1,0:T(8,128)(2,1)S(1)}, u32[]{:S(2)}, u32[]{:S(2)}) %collective-permute-start.5) | collective-permute-done | bytes 32800 | tf_op jit(solution)/shard_map/ppermute | solution.py:28
  27.9 0.1 collective-permute-done.6.p1
  28.0 2.4 %collective-permute-done.7.m1 = bf16[2,32,256]{2,1,0:T(8,128)(2,1)S(1)} collective-permute-done((bf16[2,32,256]{2,1,0:T(8,128)(2,1)S(1)}, bf16[2,32,256]{2,1,0:T(8,128)(2,1)S(1)}, u32[]{:S(2)}, u32[]{:S(2)}) %collective-permute-start.7) | collective-permute-done | bytes 32800 | tf_op jit(solution)/shard_map/ppermute | solution.py:28
  30.4 0.1 shard_map.58.x0
  30.5 2.7 %collective-permute-start.10 = (bf16[2,4,32,256]{3,2,1,0:T(8,128)(2,1)S(1)}, bf16[2,4,32,256]{3,2,1,0:T(8,128)(2,1)S(1)}, u32[]{:S(2)}, u32[]{:S(2)}) collective-permute-start(bf16[2,4,32,256]{3,2,1,0:T(8,128)(2,1)S(1)} %shard_map.58.x0), channel_id=1, source_target_pairs={{0,3},{1,0},{2,1},{3,2},{4,7},{5,4},{6,5},{7,6},{8,11},{9,8},{10,9... | collective-permute-start | bytes 393224 | tf_op jit(solution)/shard_map/ppermute | solution.py:28
  33.2 0.0 collective-permute-start.9
  33.2 1.3 %collective-permute-start.8 = (bf16[2,4,32,256]{3,2,1,0:T(8,128)(2,1)S(1)}, bf16[2,4,32,256]{3,2,1,0:T(8,128)(2,1)S(1)}, u32[]{:S(2)}, u32[]{:S(2)}) collective-permute-start(bf16[2,4,32,256]{3,2,1,0:T(8,128)(2,1)S(1)} %shard_map.58.x0), channel_id=1, source_target_pairs={{0,2},{1,3},{2,0},{3,1},{4,6},{5,7},{6,4},{7,5},{8,10},{9,11},{10,... | collective-permute-start | bytes 393224 | tf_op jit(solution)/shard_map/ppermute | solution.py:28
  34.5 0.7 %collective-permute-done.10.x3 = bf16[2,4,32,256]{3,2,1,0:T(8,128)(2,1)S(1)} collective-permute-done((bf16[2,4,32,256]{3,2,1,0:T(8,128)(2,1)S(1)}, bf16[2,4,32,256]{3,2,1,0:T(8,128)(2,1)S(1)}, u32[]{:S(2)}, u32[]{:S(2)}) %collective-permute-start.10) | collective-permute-done | bytes 131104 | tf_op jit(solution)/shard_map/ppermute | solution.py:28
  35.2 5.0 %collective-permute-done.9.x2 = bf16[2,4,32,256]{3,2,1,0:T(8,128)(2,1)S(1)} collective-permute-done((bf16[2,4,32,256]{3,2,1,0:T(8,128)(2,1)S(1)}, bf16[2,4,32,256]{3,2,1,0:T(8,128)(2,1)S(1)}, u32[]{:S(2)}, u32[]{:S(2)}) %collective-permute-start.9) | collective-permute-done | bytes 131104 | tf_op jit(solution)/shard_map/ppermute | solution.py:28
  40.1 0.0 collective-permute-done.8.x1
  40.1 9.9 %shard_map.59 = f32[2,512,256]{2,1,0:T(8,128)} custom-call(s32[64]{0:T(128)S(1)} %copy-done, bf16[2,4,32,256]{3,2,1,0:T(8,128)(2,1)S(1)} %shard_map.58.x0, bf16[2,4,32,256]{3,2,1,0:T(8,128)(2,1)S(1)} %collective-permute-done.8.x1, bf16[2,4,32,256]{3,2,1,0:T(8,128)(2,1)S(1)} %collective-permute-done.9.x2, bf16[2,4,32,256]{3,2,1,0:T(8,128)(2,1)S(1)} %collective-permute-done.10.x3), custom_call_target="tpu_custom_call" | custom-call | tf_op jit(solution)/shard_map/pallas_call | solution.py:254
Async XLA Ops:
  1.8 12.5 %copy-start = (s32[64]{0:T(128)S(1)}, s32[64]{0:T(128)}, u32[]{:S(2)}) copy-start(s32[64]{0:T(128)} %owner.3) | copy-start | bytes 772
  1.8 12.5 %copy-start.1 = (s32[5]{0:T(128)S(1)}, s32[5]{0:T(128)}, u32[]{:S(2)}) copy-start(s32[5]{0:T(128)} %port.1) | copy-start | bytes 64
  1.8 9.8 %collective-permute-start.1 = (f32[5,32,256]{2,1,0:T(8,128)S(1)}, f32[5,32,256]{2,1,0:T(8,128)S(1)}, u32[]{:S(2)}, u32[]{:S(2)}) collective-permute-start(f32[5,32,256]{2,1,0:T(8,128)S(1)} %shard_map.56), channel_id=1, source_target_pairs={{0,2},{1,3},{2,0},{3,1},{4,6},{5,7},{6,4},{7,5},{8,10},{9,11},{10,... | collective-permute-start | bytes 491528 | tf_op jit(solution)/shard_map/ppermute | solution.py:28
  8.2 6.0 %collective-permute-start = (f32[5,32,256]{2,1,0:T(8,128)S(1)}, f32[5,32,256]{2,1,0:T(8,128)S(1)}, u32[]{:S(2)}, u32[]{:S(2)}) collective-permute-start(f32[5,32,256]{2,1,0:T(8,128)S(1)} %get-tuple-element.15), channel_id=1, source_target_pairs={{0,1},{1,2},{2,3},{3,0},{4,5},{5,6},{6,7},{7,4},{8,9},{9,10},{10,1... | collective-permute-start | bytes 491528 | tf_op jit(solution)/shard_map/ppermute | solution.py:28
  8.6 5.6 %collective-permute-start.2 = (f32[5,32,256]{2,1,0:T(8,128)S(1)}, f32[5,32,256]{2,1,0:T(8,128)S(1)}, u32[]{:S(2)}, u32[]{:S(2)}) collective-permute-start(f32[5,32,256]{2,1,0:T(8,128)S(1)} %get-tuple-element.16), channel_id=1, source_target_pairs={{0,3},{1,0},{2,1},{3,2},{4,7},{5,4},{6,5},{7,6},{8,11},{9,8},{10,9... | collective-permute-start | bytes 491528 | tf_op jit(solution)/shard_map/ppermute | solution.py:28
  14.9 12.4 %collective-permute-start.3 = (bf16[2,32,256]{2,1,0:T(8,128)(2,1)S(1)}, bf16[2,32,256]{2,1,0:T(8,128)(2,1)S(1)}, u32[]{:S(2)}, u32[]{:S(2)}) collective-permute-start(bf16[2,32,256]{2,1,0:T(8,128)(2,1)S(1)} %get-tuple-element.17), channel_id=1, source_target_pairs={{0,8},{4,12},{8,16},{12,20},{16,24},{20,28},{24,32},{28,36},{32,40... | collective-permute-start | bytes 98312 | tf_op jit(solution)/shard_map/ppermute | solution.py:28
  16.3 11.0 %collective-permute-start.4 = (bf16[2,32,256]{2,1,0:T(8,128)(2,1)S(1)}, bf16[2,32,256]{2,1,0:T(8,128)(2,1)S(1)}, u32[]{:S(2)}, u32[]{:S(2)}) collective-permute-start(bf16[2,32,256]{2,1,0:T(8,128)(2,1)S(1)} %get-tuple-element.18), channel_id=1, source_target_pairs={{0,248},{4,252},{8,0},{12,4},{16,8},{20,12},{24,16},{28,20},{32,24... | collective-permute-start | bytes 98312 | tf_op jit(solution)/shard_map/ppermute | solution.py:28
  23.1 4.8 %collective-permute-start.5 = (bf16[2,32,256]{2,1,0:T(8,128)(2,1)S(1)}, bf16[2,32,256]{2,1,0:T(8,128)(2,1)S(1)}, u32[]{:S(2)}, u32[]{:S(2)}) collective-permute-start(bf16[2,32,256]{2,1,0:T(8,128)(2,1)S(1)} %get-tuple-element.19), channel_id=1, source_target_pairs={{0,244},{4,248},{8,252},{12,0},{16,4},{20,8},{24,12},{28,16},{32,2... | collective-permute-start | bytes 98312 | tf_op jit(solution)/shard_map/ppermute | solution.py:28
  26.8 1.2 %collective-permute-start.6 = (bf16[2,32,256]{2,1,0:T(8,128)(2,1)S(1)}, bf16[2,32,256]{2,1,0:T(8,128)(2,1)S(1)}, u32[]{:S(2)}, u32[]{:S(2)}) collective-permute-start(bf16[2,32,256]{2,1,0:T(8,128)(2,1)S(1)} %get-tuple-element.20), channel_id=1, source_target_pairs={{0,4},{4,8},{8,12},{12,16},{16,20},{20,24},{24,28},{28,32},{32,36}... | collective-permute-start | bytes 98312 | tf_op jit(solution)/shard_map/ppermute | solution.py:28
  26.8 3.6 %collective-permute-start.7 = (bf16[2,32,256]{2,1,0:T(8,128)(2,1)S(1)}, bf16[2,32,256]{2,1,0:T(8,128)(2,1)S(1)}, u32[]{:S(2)}, u32[]{:S(2)}) collective-permute-start(bf16[2,32,256]{2,1,0:T(8,128)(2,1)S(1)} %get-tuple-element.21), channel_id=1, source_target_pairs={{0,252},{4,0},{8,4},{12,8},{16,12},{20,16},{24,20},{28,24},{32,28}... | collective-permute-start | bytes 98312 | tf_op jit(solution)/shard_map/ppermute | solution.py:28
  30.5 4.7 %collective-permute-start.10 = (bf16[2,4,32,256]{3,2,1,0:T(8,128)(2,1)S(1)}, bf16[2,4,32,256]{3,2,1,0:T(8,128)(2,1)S(1)}, u32[]{:S(2)}, u32[]{:S(2)}) collective-permute-start(bf16[2,4,32,256]{3,2,1,0:T(8,128)(2,1)S(1)} %shard_map.58.x0), channel_id=1, source_target_pairs={{0,3},{1,0},{2,1},{3,2},{4,7},{5,4},{6,5},{7,6},{8,11},{9,8},{10,9... | collective-permute-start | bytes 393224 | tf_op jit(solution)/shard_map/ppermute | solution.py:28
  33.2 6.9 %collective-permute-start.9 = (bf16[2,4,32,256]{3,2,1,0:T(8,128)(2,1)S(1)}, bf16[2,4,32,256]{3,2,1,0:T(8,128)(2,1)S(1)}, u32[]{:S(2)}, u32[]{:S(2)}) collective-permute-start(bf16[2,4,32,256]{3,2,1,0:T(8,128)(2,1)S(1)} %shard_map.58.x0), channel_id=1, source_target_pairs={{0,1},{1,2},{2,3},{3,0},{4,5},{5,6},{6,7},{7,4},{8,9},{9,10},{10,1... | collective-permute-start | bytes 393224 | tf_op jit(solution)/shard_map/ppermute | solution.py:28
  33.2 6.9 %collective-permute-start.8 = (bf16[2,4,32,256]{3,2,1,0:T(8,128)(2,1)S(1)}, bf16[2,4,32,256]{3,2,1,0:T(8,128)(2,1)S(1)}, u32[]{:S(2)}, u32[]{:S(2)}) collective-permute-start(bf16[2,4,32,256]{3,2,1,0:T(8,128)(2,1)S(1)} %shard_map.58.x0), channel_id=1, source_target_pairs={{0,2},{1,3},{2,0},{3,1},{4,6},{5,7},{6,4},{7,5},{8,10},{9,11},{10,... | collective-permute-start | bytes 393224 | tf_op jit(solution)/shard_map/ppermute | solution.py:28

commit v5 on v4

--- a/solution.py
+++ b/solution.py
@@ -19,7 +19,7 @@
 ANY = pl.BlockSpec(memory_space=pltpu.HBM)
 PARAMS = pltpu.CompilerParams(vmem_limit_bytes=24 << 20)
 WIDE = pltpu.CompilerParams(vmem_limit_bytes=54300 << 10)
-TURNS = (0, 2, 1, 3)
+TURNS = (0, 3, 1, 2)
 ROUTES = (2, -2, -3, 1, -1)
 
 
@@ -211,10 +211,37 @@
         g = g + (0.1 * jnp.sum(g * eye) / n + 1e-6) * eye
         blocks.append([g[k * B : (k + 1) * B] for k in range(n // B)])
     col, row = col[:B], row[:B]
+    stores = []
+
+    def finish(k):
+        wide = 2 * B
+        here = pl.ds((k - 1) * B, wide)
+        depth = (k + 1) * B
+        for p in range(2):
+            w = [jnp.where(col <= row + i * B, blocks[p][i], 0.0) for i in (k - 1, k)]
+            w = jnp.concatenate(w, axis=0)[:, :depth]
+            w0 = w.astype(bf16)
+            e = w - w0.astype(f32)
+            w1 = e.astype(bf16)
+            w2 = (e - w1.astype(f32)).astype(bf16)
+            x = x_ref[p, :, :depth]
+            y = mm(x, w2, ((1,), (1,)), None) + mm(x, w1, ((1,), (1,)), None)
+            y = y + mm(x, w0, ((1,), (1,)), None)
+            for t in range(QUARTERS):
+                q = lax.rem(s - TURNS[t] + QUARTERS, QUARTERS)
+                for j in range(FACES):
+                    at = pl.multiple_of(j * QUARTERS * rows + q * rows, rows)
+                    o_ref[p, pl.ds(at, rows), here] = y[t * each + j * rows : t * each + (j + 1) * rows]
+            store = pltpu.make_async_copy(
+                o_ref.at[p, :, here], o_hbm.at[slots[p], :, here], sem.at[p, k // 2]
+            )
+            store.start()
+            stores.append(store)
+
     for k in range(n // B):
         lo, hi = k * B, (k + 1) * B
         inside = (col >= lo) & (col < hi)
-        t = panel(jnp.concatenate([s[k][:, lo:hi] for s in blocks], axis=1))
+        t = panel(jnp.concatenate([x[k][:, lo:hi] for x in blocks], axis=1))
         ys = []
         for p in range(2):
             w = t[:, p * B : (p + 1) * B]
@@ -225,25 +252,8 @@
             for p in range(2):
                 u = mm(blocks[p][i][:, lo:hi], ys[p], ((1,), (1,)))
                 blocks[p][i] = jnp.where(inside, 0.0, blocks[p][i]) - mm(u, blocks[p][k])
-    stores = []
-    for p in range(2):
-        w = [jnp.where(col <= row + k * B, s, 0.0) for k, s in enumerate(blocks[p])]
-        w = jnp.concatenate(w, axis=0)
-        w0 = w.astype(bf16)
-        e = w - w0.astype(f32)
-        w1 = e.astype(bf16)
-        w2 = (e - w1.astype(f32)).astype(bf16)
-        x = x_ref[p]
-        acc = mm(x, w2, ((1,), (1,)), None) + mm(x, w1, ((1,), (1,)), None)
-        y = acc + mm(x, w0, ((1,), (1,)), None)
-        for k in range(QUARTERS):
-            q = lax.rem(s - TURNS[k] + QUARTERS, QUARTERS)
-            for j in range(FACES):
-                at = pl.multiple_of(j * QUARTERS * rows + q * rows, rows)
-                o_ref[p, pl.ds(at, rows), :] = y[k * each + j * rows : k * each + (j + 1) * rows]
-        store = pltpu.make_async_copy(o_ref.at[p], o_hbm.at[slots[p]], sem.at[p])
-        store.start()
-        stores.append(store)
+        if k % 2:
+            finish(k)
     for store in stores:
         store.wait()
 
@@ -259,7 +269,7 @@
         scratch_shapes=[
             pltpu.VMEM((2, height, n), bf16),
             pltpu.VMEM((2, height, n), f32),
-            pltpu.SemaphoreType.DMA((2,)),
+            pltpu.SemaphoreType.DMA((2, 2)),
         ],
         compiler_params=PARAMS,
     )(port_owner, *pieces)

time: 50.6 us -> 49.6 us (0.980)
  waiting for transfers between devices: 11.4 us -> 10.5 us
    ppermute x11, waiting for transfers between devices: 11.4 us -> 10.5 us  [shifted(): lax.ppermute(block, axis, [(i, (i + distance) % n) for i in range(n)])]
  transfers between devices with their start and end apart: 11 -> 11, of which waited for: 6 -> 7; matrix products, arithmetic and copies ran while one was open for 0% -> 0% of each run, Pallas kernels for 5% -> 6%
where the time goes in v5:
time: 49.6 us; the launch traced here: 48.8 us
  starting transfers between devices  22.5 us (45%)
  Pallas kernels  14.9 us (30%)
  waiting for transfers between devices  10.5 us (21%)
  between operations  0.88 us (2%)
    ppermute x11, starting transfers between devices, shifted(): lax.ppermute(block, axis, [(i, (i + distance) % n) for i in range(n)])  22.5 us
    ppermute x11, waiting for transfers between devices, shifted(): lax.ppermute(block, axis, [(i, (i + distance) % n) for i in range(n)])  10.5 us
    pallas_call x1, Pallas kernels, solve(): pl.pallas_call(solve_kernel, out_shape=jax.ShapeDtypeStruct((2, height, n...  9.68 us
    pallas_call x2, Pallas kernels, sketch_parts(): pl.pallas_call(functools.partial(sketch_kernel, turns), out_shape=[part]...  4.51 us
  transfers between devices with their start and end apart: 11, of which 7 were waited for; matrix products, arithmetic and copies ran while one was open for 0% of the time, Pallas kernels for 6%

profile of v5, /device:TPU:1, one launch (start us, length us, event | category | flops | bytes accessed | tf_op | source)
XLA Modules:
  0.0 48.8 jit_solution(805104107778459730)
XLA Ops:
  0.0 1.8 %shard_map.56 = f32[5,32,256]{2,1,0:T(8,128)S(1)} custom-call(bf16[5,128,2048]{2,1,0:T(8,128)(2,1)} %t_hbm.3, bf16[2048,256]{1,0:T(8,128)(2,1)} %r_hbm.3), custom_call_target="tpu_custom_call" | custom-call | tf_op jit(solution)/shard_map/pallas_call | solution.py:61
  1.8 0.0 copy-start
  1.8 0.0 copy-start.1
  1.8 3.7 %collective-permute-start.1 = (f32[5,32,256]{2,1,0:T(8,128)S(1)}, f32[5,32,256]{2,1,0:T(8,128)S(1)}, u32[]{:S(2)}, u32[]{:S(2)}) collective-permute-start(f32[5,32,256]{2,1,0:T(8,128)S(1)} %shard_map.56), channel_id=1, source_target_pairs={{0,2},{1,3},{2,0},{3,1},{4,6},{5,7},{6,4},{7,5},{8,10},{9,11},{10,... | collective-permute-start | bytes 491528 | tf_op jit(solution)/shard_map/ppermute | solution.py:28
  5.5 2.8 %shard_map.55 = (f32[5,32,256]{2,1,0:T(8,128)S(1)}, f32[5,32,256]{2,1,0:T(8,128)S(1)}, f32[5,32,256]{2,1,0:T(8,128)S(1)}) custom-call(bf16[5,128,2048]{2,1,0:T(8,128)(2,1)} %t_hbm.3, bf16[2048,256]{1,0:T(8,128)(2,1)} %r_hbm.3), custom_call_target="tpu_custom_call" | custom-call | tf_op jit(solution)/shard_map/pallas_call | solution.py:61
  8.2 0.4 collective-permute-start
  8.6 2.4 %collective-permute-start.2 = (f32[5,32,256]{2,1,0:T(8,128)S(1)}, f32[5,32,256]{2,1,0:T(8,128)S(1)}, u32[]{:S(2)}, u32[]{:S(2)}) collective-permute-start(f32[5,32,256]{2,1,0:T(8,128)S(1)} %get-tuple-element.16), channel_id=1, source_target_pairs={{0,3},{1,0},{2,1},{3,2},{4,7},{5,4},{6,5},{7,6},{8,11},{9,8},{10,9... | collective-permute-start | bytes 491528 | tf_op jit(solution)/shard_map/ppermute | solution.py:28
  11.6 0.0 collective-permute-done.1.c
  11.6 2.6 %collective-permute-done.b = f32[5,32,256]{2,1,0:T(8,128)S(1)} collective-permute-done((f32[5,32,256]{2,1,0:T(8,128)S(1)}, f32[5,32,256]{2,1,0:T(8,128)S(1)}, u32[]{:S(2)}, u32[]{:S(2)}) %collective-permute-start) | collective-permute-done | bytes 163872 | tf_op jit(solution)/shard_map/ppermute | solution.py:28
  14.2 0.0 collective-permute-done.2.d
  14.2 0.0 copy-done
  14.3 0.0 copy-done.1
  14.3 0.6 %shard_map.57 = (bf16[2,32,256]{2,1,0:T(8,128)(2,1)S(1)}, bf16[2,32,256]{2,1,0:T(8,128)(2,1)S(1)}, bf16[2,32,256]{2,1,0:T(8,128)(2,1)S(1)}, bf16[2,32,256]{2,1,0...) custom-call(s32[5]{0:T(128)S(1)} %copy-done.1, s32[1]{0:T(128)S(6)} %copy.6.count, ...), custom_call_target="tpu_custom_call" | custom-call | tf_op jit(solution)/shard_map/pallas_call | solution.py:105
  14.9 1.4 %collective-permute-start.3 = (bf16[2,32,256]{2,1,0:T(8,128)(2,1)S(1)}, bf16[2,32,256]{2,1,0:T(8,128)(2,1)S(1)}, u32[]{:S(2)}, u32[]{:S(2)}) collective-permute-start(bf16[2,32,256]{2,1,0:T(8,128)(2,1)S(1)} %get-tuple-element.17), channel_id=1, source_target_pairs={{0,8},{4,12},{8,16},{12,20},{16,24},{20,28},{24,32},{28,36},{32,40... | collective-permute-start | bytes 98312 | tf_op jit(solution)/shard_map/ppermute | solution.py:28
  16.3 6.8 %collective-permute-start.4 = (bf16[2,32,256]{2,1,0:T(8,128)(2,1)S(1)}, bf16[2,32,256]{2,1,0:T(8,128)(2,1)S(1)}, u32[]{:S(2)}, u32[]{:S(2)}) collective-permute-start(bf16[2,32,256]{2,1,0:T(8,128)(2,1)S(1)} %get-tuple-element.18), channel_id=1, source_target_pairs={{0,248},{4,252},{8,0},{12,4},{16,8},{20,12},{24,16},{28,20},{32,24... | collective-permute-start | bytes 98312 | tf_op jit(solution)/shard_map/ppermute | solution.py:28
  23.1 3.7 %collective-permute-start.5 = (bf16[2,32,256]{2,1,0:T(8,128)(2,1)S(1)}, bf16[2,32,256]{2,1,0:T(8,128)(2,1)S(1)}, u32[]{:S(2)}, u32[]{:S(2)}) collective-permute-start(bf16[2,32,256]{2,1,0:T(8,128)(2,1)S(1)} %get-tuple-element.19), channel_id=1, source_target_pairs={{0,244},{4,248},{8,252},{12,0},{16,4},{20,8},{24,12},{28,16},{32,2... | collective-permute-start | bytes 98312 | tf_op jit(solution)/shard_map/ppermute | solution.py:28
  26.8 0.0 collective-permute-start.6
  26.8 0.5 %collective-permute-start.7 = (bf16[2,32,256]{2,1,0:T(8,128)(2,1)S(1)}, bf16[2,32,256]{2,1,0:T(8,128)(2,1)S(1)}, u32[]{:S(2)}, u32[]{:S(2)}) collective-permute-start(bf16[2,32,256]{2,1,0:T(8,128)(2,1)S(1)} %get-tuple-element.21), channel_id=1, source_target_pairs={{0,252},{4,0},{8,4},{12,8},{16,12},{20,16},{24,20},{28,24},{32,28}... | collective-permute-start | bytes 98312 | tf_op jit(solution)/shard_map/ppermute | solution.py:28
  27.3 0.0 collective-permute-done.3.p2
  27.3 0.0 collective-permute-done.4.m2
  27.3 0.6 %collective-permute-done.5.m3 = bf16[2,32,256]{2,1,0:T(8,128)(2,1)S(1)} collective-permute-done((bf16[2,32,256]{2,1,0:T(8,128)(2,1)S(1)}, bf16[2,32,256]{2,1,0:T(8,128)(2,1)S(1)}, u32[]{:S(2)}, u32[]{:S(2)}) %collective-permute-start.5) | collective-permute-done | bytes 32800 | tf_op jit(solution)/shard_map/ppermute | solution.py:28
  27.9 0.1 collective-permute-done.6.p1
  28.0 2.4 %collective-permute-done.7.m1 = bf16[2,32,256]{2,1,0:T(8,128)(2,1)S(1)} collective-permute-done((bf16[2,32,256]{2,1,0:T(8,128)(2,1)S(1)}, bf16[2,32,256]{2,1,0:T(8,128)(2,1)S(1)}, u32[]{:S(2)}, u32[]{:S(2)}) %collective-permute-start.7) | collective-permute-done | bytes 32800 | tf_op jit(solution)/shard_map/ppermute | solution.py:28
  30.4 0.1 shard_map.58.x0
  30.5 1.0 %collective-permute-start.10 = (bf16[2,4,32,256]{3,2,1,0:T(8,128)(2,1)S(1)}, bf16[2,4,32,256]{3,2,1,0:T(8,128)(2,1)S(1)}, u32[]{:S(2)}, u32[]{:S(2)}) collective-permute-start(bf16[2,4,32,256]{3,2,1,0:T(8,128)(2,1)S(1)} %shard_map.58.x0), channel_id=1, source_target_pairs={{0,2},{1,3},{2,0},{3,1},{4,6},{5,7},{6,4},{7,5},{8,10},{9,11},{10,... | collective-permute-start | bytes 393224 | tf_op jit(solution)/shard_map/ppermute | solution.py:28
  31.4 2.4 %collective-permute-start.9 = (bf16[2,4,32,256]{3,2,1,0:T(8,128)(2,1)S(1)}, bf16[2,4,32,256]{3,2,1,0:T(8,128)(2,1)S(1)}, u32[]{:S(2)}, u32[]{:S(2)}) collective-permute-start(bf16[2,4,32,256]{3,2,1,0:T(8,128)(2,1)S(1)} %shard_map.58.x0), channel_id=1, source_target_pairs={{0,1},{1,2},{2,3},{3,0},{4,5},{5,6},{6,7},{7,4},{8,9},{9,10},{10,1... | collective-permute-start | bytes 393224 | tf_op jit(solution)/shard_map/ppermute | solution.py:28
  33.8 0.3 collective-permute-start.8
  34.1 1.9 %collective-permute-done.10.x3 = bf16[2,4,32,256]{3,2,1,0:T(8,128)(2,1)S(1)} collective-permute-done((bf16[2,4,32,256]{3,2,1,0:T(8,128)(2,1)S(1)}, bf16[2,4,32,256]{3,2,1,0:T(8,128)(2,1)S(1)}, u32[]{:S(2)}, u32[]{:S(2)}) %collective-permute-start.10) | collective-permute-done | bytes 131104 | tf_op jit(solution)/shard_map/ppermute | solution.py:28
  36.0 2.4 %collective-permute-done.9.x2 = bf16[2,4,32,256]{3,2,1,0:T(8,128)(2,1)S(1)} collective-permute-done((bf16[2,4,32,256]{3,2,1,0:T(8,128)(2,1)S(1)}, bf16[2,4,32,256]{3,2,1,0:T(8,128)(2,1)S(1)}, u32[]{:S(2)}, u32[]{:S(2)}) %collective-permute-start.9) | collective-permute-done | bytes 131104 | tf_op jit(solution)/shard_map/ppermute | solution.py:28
  38.4 0.5 %collective-permute-done.8.x1 = bf16[2,4,32,256]{3,2,1,0:T(8,128)(2,1)S(1)} collective-permute-done((bf16[2,4,32,256]{3,2,1,0:T(8,128)(2,1)S(1)}, bf16[2,4,32,256]{3,2,1,0:T(8,128)(2,1)S(1)}, u32[]{:S(2)}, u32[]{:S(2)}) %collective-permute-start.8) | collective-permute-done | bytes 131104 | tf_op jit(solution)/shard_map/ppermute | solution.py:28
  38.9 9.7 %shard_map.59 = f32[2,512,256]{2,1,0:T(8,128)} custom-call(s32[64]{0:T(128)S(1)} %copy-done, bf16[2,4,32,256]{3,2,1,0:T(8,128)(2,1)S(1)} %shard_map.58.x0, bf16[2,4,32,256]{3,2,1,0:T(8,128)(2,1)S(1)} %collective-permute-done.8.x1, bf16[2,4,32,256]{3,2,1,0:T(8,128)(2,1)S(1)} %collective-permute-done.9.x2, bf16[2,4,32,256]{3,2,1,0:T(8,128)(2,1)S(1)} %collective-permute-done.10.x3), custom_call_target="tpu_custom_call" | custom-call | tf_op jit(solution)/shard_map/pallas_call | solution.py:264
Async XLA Ops:
  1.8 12.5 %copy-start = (s32[64]{0:T(128)S(1)}, s32[64]{0:T(128)}, u32[]{:S(2)}) copy-start(s32[64]{0:T(128)} %owner.3) | copy-start | bytes 772
  1.8 12.5 %copy-start.1 = (s32[5]{0:T(128)S(1)}, s32[5]{0:T(128)}, u32[]{:S(2)}) copy-start(s32[5]{0:T(128)} %port.1) | copy-start | bytes 64
  1.8 9.8 %collective-permute-start.1 = (f32[5,32,256]{2,1,0:T(8,128)S(1)}, f32[5,32,256]{2,1,0:T(8,128)S(1)}, u32[]{:S(2)}, u32[]{:S(2)}) collective-permute-start(f32[5,32,256]{2,1,0:T(8,128)S(1)} %shard_map.56), channel_id=1, source_target_pairs={{0,2},{1,3},{2,0},{3,1},{4,6},{5,7},{6,4},{7,5},{8,10},{9,11},{10,... | collective-permute-start | bytes 491528 | tf_op jit(solution)/shard_map/ppermute | solution.py:28
  8.2 6.0 %collective-permute-start = (f32[5,32,256]{2,1,0:T(8,128)S(1)}, f32[5,32,256]{2,1,0:T(8,128)S(1)}, u32[]{:S(2)}, u32[]{:S(2)}) collective-permute-start(f32[5,32,256]{2,1,0:T(8,128)S(1)} %get-tuple-element.15), channel_id=1, source_target_pairs={{0,1},{1,2},{2,3},{3,0},{4,5},{5,6},{6,7},{7,4},{8,9},{9,10},{10,1... | collective-permute-start | bytes 491528 | tf_op jit(solution)/shard_map/ppermute | solution.py:28
  8.6 5.6 %collective-permute-start.2 = (f32[5,32,256]{2,1,0:T(8,128)S(1)}, f32[5,32,256]{2,1,0:T(8,128)S(1)}, u32[]{:S(2)}, u32[]{:S(2)}) collective-permute-start(f32[5,32,256]{2,1,0:T(8,128)S(1)} %get-tuple-element.16), channel_id=1, source_target_pairs={{0,3},{1,0},{2,1},{3,2},{4,7},{5,4},{6,5},{7,6},{8,11},{9,8},{10,9... | collective-permute-start | bytes 491528 | tf_op jit(solution)/shard_map/ppermute | solution.py:28
  14.9 12.4 %collective-permute-start.3 = (bf16[2,32,256]{2,1,0:T(8,128)(2,1)S(1)}, bf16[2,32,256]{2,1,0:T(8,128)(2,1)S(1)}, u32[]{:S(2)}, u32[]{:S(2)}) collective-permute-start(bf16[2,32,256]{2,1,0:T(8,128)(2,1)S(1)} %get-tuple-element.17), channel_id=1, source_target_pairs={{0,8},{4,12},{8,16},{12,20},{16,24},{20,28},{24,32},{28,36},{32,40... | collective-permute-start | bytes 98312 | tf_op jit(solution)/shard_map/ppermute | solution.py:28
  16.3 11.0 %collective-permute-start.4 = (bf16[2,32,256]{2,1,0:T(8,128)(2,1)S(1)}, bf16[2,32,256]{2,1,0:T(8,128)(2,1)S(1)}, u32[]{:S(2)}, u32[]{:S(2)}) collective-permute-start(bf16[2,32,256]{2,1,0:T(8,128)(2,1)S(1)} %get-tuple-element.18), channel_id=1, source_target_pairs={{0,248},{4,252},{8,0},{12,4},{16,8},{20,12},{24,16},{28,20},{32,24... | collective-permute-start | bytes 98312 | tf_op jit(solution)/shard_map/ppermute | solution.py:28
  23.1 4.8 %collective-permute-start.5 = (bf16[2,32,256]{2,1,0:T(8,128)(2,1)S(1)}, bf16[2,32,256]{2,1,0:T(8,128)(2,1)S(1)}, u32[]{:S(2)}, u32[]{:S(2)}) collective-permute-start(bf16[2,32,256]{2,1,0:T(8,128)(2,1)S(1)} %get-tuple-element.19), channel_id=1, source_target_pairs={{0,244},{4,248},{8,252},{12,0},{16,4},{20,8},{24,12},{28,16},{32,2... | collective-permute-start | bytes 98312 | tf_op jit(solution)/shard_map/ppermute | solution.py:28
  26.8 1.2 %collective-permute-start.6 = (bf16[2,32,256]{2,1,0:T(8,128)(2,1)S(1)}, bf16[2,32,256]{2,1,0:T(8,128)(2,1)S(1)}, u32[]{:S(2)}, u32[]{:S(2)}) collective-permute-start(bf16[2,32,256]{2,1,0:T(8,128)(2,1)S(1)} %get-tuple-element.20), channel_id=1, source_target_pairs={{0,4},{4,8},{8,12},{12,16},{16,20},{20,24},{24,28},{28,32},{32,36}... | collective-permute-start | bytes 98312 | tf_op jit(solution)/shard_map/ppermute | solution.py:28
  26.8 3.6 %collective-permute-start.7 = (bf16[2,32,256]{2,1,0:T(8,128)(2,1)S(1)}, bf16[2,32,256]{2,1,0:T(8,128)(2,1)S(1)}, u32[]{:S(2)}, u32[]{:S(2)}) collective-permute-start(bf16[2,32,256]{2,1,0:T(8,128)(2,1)S(1)} %get-tuple-element.21), channel_id=1, source_target_pairs={{0,252},{4,0},{8,4},{12,8},{16,12},{20,16},{24,20},{28,24},{32,28}... | collective-permute-start | bytes 98312 | tf_op jit(solution)/shard_map/ppermute | solution.py:28
  30.5 5.5 %collective-permute-start.10 = (bf16[2,4,32,256]{3,2,1,0:T(8,128)(2,1)S(1)}, bf16[2,4,32,256]{3,2,1,0:T(8,128)(2,1)S(1)}, u32[]{:S(2)}, u32[]{:S(2)}) collective-permute-start(bf16[2,4,32,256]{3,2,1,0:T(8,128)(2,1)S(1)} %shard_map.58.x0), channel_id=1, source_target_pairs={{0,2},{1,3},{2,0},{3,1},{4,6},{5,7},{6,4},{7,5},{8,10},{9,11},{10,... | collective-permute-start | bytes 393224 | tf_op jit(solution)/shard_map/ppermute | solution.py:28
  31.4 6.9 %collective-permute-start.9 = (bf16[2,4,32,256]{3,2,1,0:T(8,128)(2,1)S(1)}, bf16[2,4,32,256]{3,2,1,0:T(8,128)(2,1)S(1)}, u32[]{:S(2)}, u32[]{:S(2)}) collective-permute-start(bf16[2,4,32,256]{3,2,1,0:T(8,128)(2,1)S(1)} %shard_map.58.x0), channel_id=1, source_target_pairs={{0,1},{1,2},{2,3},{3,0},{4,5},{5,6},{6,7},{7,4},{8,9},{9,10},{10,1... | collective-permute-start | bytes 393224 | tf_op jit(solution)/shard_map/ppermute | solution.py:28
  33.8 5.1 %collective-permute-start.8 = (bf16[2,4,32,256]{3,2,1,0:T(8,128)(2,1)S(1)}, bf16[2,4,32,256]{3,2,1,0:T(8,128)(2,1)S(1)}, u32[]{:S(2)}, u32[]{:S(2)}) collective-permute-start(bf16[2,4,32,256]{3,2,1,0:T(8,128)(2,1)S(1)} %shard_map.58.x0), channel_id=1, source_target_pairs={{0,3},{1,0},{2,1},{3,2},{4,7},{5,4},{6,5},{7,6},{8,11},{9,8},{10,9... | collective-permute-start | bytes 393224 | tf_op jit(solution)/shard_map/ppermute | solution.py:28

commit v6 on v5

--- a/solution.py
+++ b/solution.py
@@ -188,14 +188,12 @@
     return jnp.concatenate(rows, axis=0)
 
 
-def solve_kernel(owner, x0, x1, x2, x3, o_hbm, x_ref, o_ref, sem):
+def solve_kernel(owner_hbm, x0, x1, x2, x3, o_hbm, x_ref, o_ref, owner, sem, owner_sem):
+    table = pltpu.make_async_copy(owner_hbm, owner, owner_sem)
+    table.start()
     me = lax.axis_index("mesh")
     s = lax.axis_index("samp")
-    ports = owner.shape[0]
-    near, far = lax.rem(me - 1 + ports, ports), lax.rem(me - 2 + ports, ports)
-    both = (owner[near] == me) & (owner[far] == me)
-    near_first = jnp.where(both, near < far, owner[near] == me)
-    slots = (jnp.where(near_first, 0, 1), jnp.where(near_first, 1, 0))
+    slots = []
     n = x0.shape[3]
     rows = x0.shape[2]
     each = FACES * rows
@@ -252,6 +250,13 @@
             for p in range(2):
                 u = mm(blocks[p][i][:, lo:hi], ys[p], ((1,), (1,)))
                 blocks[p][i] = jnp.where(inside, 0.0, blocks[p][i]) - mm(u, blocks[p][k])
+        if k == 1:
+            table.wait()
+            ports = owner.shape[0]
+            near, far = lax.rem(me - 1 + ports, ports), lax.rem(me - 2 + ports, ports)
+            both = (owner[near] == me) & (owner[far] == me)
+            near_first = jnp.where(both, near < far, owner[near] == me)
+            slots += [jnp.where(near_first, 0, 1), jnp.where(near_first, 1, 0)]
         if k % 2:
             finish(k)
     for store in stores:
@@ -264,12 +269,14 @@
     return pl.pallas_call(
         solve_kernel,
         out_shape=jax.ShapeDtypeStruct((2, height, n), f32),
-        in_specs=[SM] + [VM] * QUARTERS,
+        in_specs=[ANY] + [VM] * QUARTERS,
         out_specs=ANY,
         scratch_shapes=[
             pltpu.VMEM((2, height, n), bf16),
             pltpu.VMEM((2, height, n), f32),
+            pltpu.SMEM((port_owner.shape[0],), jnp.int32),
             pltpu.SemaphoreType.DMA((2, 2)),
+            pltpu.SemaphoreType.DMA,
         ],
         compiler_params=PARAMS,
     )(port_owner, *pieces)

time: 49.6 us -> 49.3 us (level)
  no operation moved by 1% of the time
where the time goes in v6:
time: 49.3 us; the launch traced here: 48.4 us
  starting transfers between devices  22.5 us (46%)
  Pallas kernels  14.5 us (29%)
  waiting for transfers between devices  10.5 us (21%)
  between operations  0.88 us (2%)
    ppermute x11, starting transfers between devices, shifted(): lax.ppermute(block, axis, [(i, (i + distance) % n) for i in range(n)])  22.5 us
    ppermute x11, waiting for transfers between devices, shifted(): lax.ppermute(block, axis, [(i, (i + distance) % n) for i in range(n)])  10.5 us
    pallas_call x1, Pallas kernels, solve(): pl.pallas_call(solve_kernel, out_shape=jax.ShapeDtypeStruct((2, height, n...  9.34 us
    pallas_call x2, Pallas kernels, sketch_parts(): pl.pallas_call(functools.partial(sketch_kernel, turns), out_shape=[part]...  4.51 us
  transfers between devices with their start and end apart: 11, of which 7 were waited for; matrix products, arithmetic and copies ran while one was open for 0% of the time, Pallas kernels for 6%

profile of v6, /device:TPU:1, one launch (start us, length us, event | category | flops | bytes accessed | tf_op | source)
XLA Modules:
  0.0 48.4 jit_solution(16835341228335494099)
XLA Ops:
  0.0 1.8 %shard_map.56 = f32[5,32,256]{2,1,0:T(8,128)S(1)} custom-call(bf16[5,128,2048]{2,1,0:T(8,128)(2,1)} %t_hbm.3, bf16[2048,256]{1,0:T(8,128)(2,1)} %r_hbm.3), custom_call_target="tpu_custom_call" | custom-call | tf_op jit(solution)/shard_map/pallas_call | solution.py:61
  1.8 0.0 copy-start
  1.8 0.0 copy-start.1
  1.8 3.7 %collective-permute-start.1 = (f32[5,32,256]{2,1,0:T(8,128)S(1)}, f32[5,32,256]{2,1,0:T(8,128)S(1)}, u32[]{:S(2)}, u32[]{:S(2)}) collective-permute-start(f32[5,32,256]{2,1,0:T(8,128)S(1)} %shard_map.56), channel_id=1, source_target_pairs={{0,2},{1,3},{2,0},{3,1},{4,6},{5,7},{6,4},{7,5},{8,10},{9,11},{10,... | collective-permute-start | bytes 491528 | tf_op jit(solution)/shard_map/ppermute | solution.py:28
  5.5 2.8 %shard_map.55 = (f32[5,32,256]{2,1,0:T(8,128)S(1)}, f32[5,32,256]{2,1,0:T(8,128)S(1)}, f32[5,32,256]{2,1,0:T(8,128)S(1)}) custom-call(bf16[5,128,2048]{2,1,0:T(8,128)(2,1)} %t_hbm.3, bf16[2048,256]{1,0:T(8,128)(2,1)} %r_hbm.3), custom_call_target="tpu_custom_call" | custom-call | tf_op jit(solution)/shard_map/pallas_call | solution.py:61
  8.2 0.4 collective-permute-start
  8.6 2.4 %collective-permute-start.2 = (f32[5,32,256]{2,1,0:T(8,128)S(1)}, f32[5,32,256]{2,1,0:T(8,128)S(1)}, u32[]{:S(2)}, u32[]{:S(2)}) collective-permute-start(f32[5,32,256]{2,1,0:T(8,128)S(1)} %get-tuple-element.16), channel_id=1, source_target_pairs={{0,3},{1,0},{2,1},{3,2},{4,7},{5,4},{6,5},{7,6},{8,11},{9,8},{10,9... | collective-permute-start | bytes 491528 | tf_op jit(solution)/shard_map/ppermute | solution.py:28
  11.6 0.0 collective-permute-done.1.c
  11.6 2.6 %collective-permute-done.b = f32[5,32,256]{2,1,0:T(8,128)S(1)} collective-permute-done((f32[5,32,256]{2,1,0:T(8,128)S(1)}, f32[5,32,256]{2,1,0:T(8,128)S(1)}, u32[]{:S(2)}, u32[]{:S(2)}) %collective-permute-start) | collective-permute-done | bytes 163872 | tf_op jit(solution)/shard_map/ppermute | solution.py:28
  14.2 0.0 collective-permute-done.2.d
  14.2 0.0 copy-done
  14.3 0.0 copy-done.1
  14.3 0.6 %shard_map.57 = (bf16[2,32,256]{2,1,0:T(8,128)(2,1)S(1)}, bf16[2,32,256]{2,1,0:T(8,128)(2,1)S(1)}, bf16[2,32,256]{2,1,0:T(8,128)(2,1)S(1)}, bf16[2,32,256]{2,1,0...) custom-call(s32[5]{0:T(128)S(1)} %copy-done.1, s32[1]{0:T(128)S(6)} %copy.6.count, ...), custom_call_target="tpu_custom_call" | custom-call | tf_op jit(solution)/shard_map/pallas_call | solution.py:105
  14.9 1.4 %collective-permute-start.3 = (bf16[2,32,256]{2,1,0:T(8,128)(2,1)S(1)}, bf16[2,32,256]{2,1,0:T(8,128)(2,1)S(1)}, u32[]{:S(2)}, u32[]{:S(2)}) collective-permute-start(bf16[2,32,256]{2,1,0:T(8,128)(2,1)S(1)} %get-tuple-element.17), channel_id=1, source_target_pairs={{0,8},{4,12},{8,16},{12,20},{16,24},{20,28},{24,32},{28,36},{32,40... | collective-permute-start | bytes 98312 | tf_op jit(solution)/shard_map/ppermute | solution.py:28
  16.3 6.8 %collective-permute-start.4 = (bf16[2,32,256]{2,1,0:T(8,128)(2,1)S(1)}, bf16[2,32,256]{2,1,0:T(8,128)(2,1)S(1)}, u32[]{:S(2)}, u32[]{:S(2)}) collective-permute-start(bf16[2,32,256]{2,1,0:T(8,128)(2,1)S(1)} %get-tuple-element.18), channel_id=1, source_target_pairs={{0,248},{4,252},{8,0},{12,4},{16,8},{20,12},{24,16},{28,20},{32,24... | collective-permute-start | bytes 98312 | tf_op jit(solution)/shard_map/ppermute | solution.py:28
  23.1 3.7 %collective-permute-start.5 = (bf16[2,32,256]{2,1,0:T(8,128)(2,1)S(1)}, bf16[2,32,256]{2,1,0:T(8,128)(2,1)S(1)}, u32[]{:S(2)}, u32[]{:S(2)}) collective-permute-start(bf16[2,32,256]{2,1,0:T(8,128)(2,1)S(1)} %get-tuple-element.19), channel_id=1, source_target_pairs={{0,244},{4,248},{8,252},{12,0},{16,4},{20,8},{24,12},{28,16},{32,2... | collective-permute-start | bytes 98312 | tf_op jit(solution)/shard_map/ppermute | solution.py:28
  26.8 0.0 collective-permute-start.6
  26.8 0.5 %collective-permute-start.7 = (bf16[2,32,256]{2,1,0:T(8,128)(2,1)S(1)}, bf16[2,32,256]{2,1,0:T(8,128)(2,1)S(1)}, u32[]{:S(2)}, u32[]{:S(2)}) collective-permute-start(bf16[2,32,256]{2,1,0:T(8,128)(2,1)S(1)} %get-tuple-element.21), channel_id=1, source_target_pairs={{0,252},{4,0},{8,4},{12,8},{16,12},{20,16},{24,20},{28,24},{32,28}... | collective-permute-start | bytes 98312 | tf_op jit(solution)/shard_map/ppermute | solution.py:28
  27.3 0.0 collective-permute-done.3.p2
  27.3 0.0 collective-permute-done.4.m2
  27.3 0.6 %collective-permute-done.5.m3 = bf16[2,32,256]{2,1,0:T(8,128)(2,1)S(1)} collective-permute-done((bf16[2,32,256]{2,1,0:T(8,128)(2,1)S(1)}, bf16[2,32,256]{2,1,0:T(8,128)(2,1)S(1)}, u32[]{:S(2)}, u32[]{:S(2)}) %collective-permute-start.5) | collective-permute-done | bytes 32800 | tf_op jit(solution)/shard_map/ppermute | solution.py:28
  27.9 0.1 collective-permute-done.6.p1
  28.0 2.4 %collective-permute-done.7.m1 = bf16[2,32,256]{2,1,0:T(8,128)(2,1)S(1)} collective-permute-done((bf16[2,32,256]{2,1,0:T(8,128)(2,1)S(1)}, bf16[2,32,256]{2,1,0:T(8,128)(2,1)S(1)}, u32[]{:S(2)}, u32[]{:S(2)}) %collective-permute-start.7) | collective-permute-done | bytes 32800 | tf_op jit(solution)/shard_map/ppermute | solution.py:28
  30.4 0.1 shard_map.58.x0
  30.5 1.0 %collective-permute-start.10 = (bf16[2,4,32,256]{3,2,1,0:T(8,128)(2,1)S(1)}, bf16[2,4,32,256]{3,2,1,0:T(8,128)(2,1)S(1)}, u32[]{:S(2)}, u32[]{:S(2)}) collective-permute-start(bf16[2,4,32,256]{3,2,1,0:T(8,128)(2,1)S(1)} %shard_map.58.x0), channel_id=1, source_target_pairs={{0,2},{1,3},{2,0},{3,1},{4,6},{5,7},{6,4},{7,5},{8,10},{9,11},{10,... | collective-permute-start | bytes 393224 | tf_op jit(solution)/shard_map/ppermute | solution.py:28
  31.4 2.4 %collective-permute-start.9 = (bf16[2,4,32,256]{3,2,1,0:T(8,128)(2,1)S(1)}, bf16[2,4,32,256]{3,2,1,0:T(8,128)(2,1)S(1)}, u32[]{:S(2)}, u32[]{:S(2)}) collective-permute-start(bf16[2,4,32,256]{3,2,1,0:T(8,128)(2,1)S(1)} %shard_map.58.x0), channel_id=1, source_target_pairs={{0,1},{1,2},{2,3},{3,0},{4,5},{5,6},{6,7},{7,4},{8,9},{9,10},{10,1... | collective-permute-start | bytes 393224 | tf_op jit(solution)/shard_map/ppermute | solution.py:28
  33.8 0.3 collective-permute-start.8
  34.1 1.9 %collective-permute-done.10.x3 = bf16[2,4,32,256]{3,2,1,0:T(8,128)(2,1)S(1)} collective-permute-done((bf16[2,4,32,256]{3,2,1,0:T(8,128)(2,1)S(1)}, bf16[2,4,32,256]{3,2,1,0:T(8,128)(2,1)S(1)}, u32[]{:S(2)}, u32[]{:S(2)}) %collective-permute-start.10) | collective-permute-done | bytes 131104 | tf_op jit(solution)/shard_map/ppermute | solution.py:28
  36.0 2.4 %collective-permute-done.9.x2 = bf16[2,4,32,256]{3,2,1,0:T(8,128)(2,1)S(1)} collective-permute-done((bf16[2,4,32,256]{3,2,1,0:T(8,128)(2,1)S(1)}, bf16[2,4,32,256]{3,2,1,0:T(8,128)(2,1)S(1)}, u32[]{:S(2)}, u32[]{:S(2)}) %collective-permute-start.9) | collective-permute-done | bytes 131104 | tf_op jit(solution)/shard_map/ppermute | solution.py:28
  38.4 0.5 %collective-permute-done.8.x1 = bf16[2,4,32,256]{3,2,1,0:T(8,128)(2,1)S(1)} collective-permute-done((bf16[2,4,32,256]{3,2,1,0:T(8,128)(2,1)S(1)}, bf16[2,4,32,256]{3,2,1,0:T(8,128)(2,1)S(1)}, u32[]{:S(2)}, u32[]{:S(2)}) %collective-permute-start.8) | collective-permute-done | bytes 131104 | tf_op jit(solution)/shard_map/ppermute | solution.py:28
  38.9 9.3 %shard_map.59 = f32[2,512,256]{2,1,0:T(8,128)} custom-call(s32[64]{0:T(128)S(1)} %copy-done, bf16[2,4,32,256]{3,2,1,0:T(8,128)(2,1)S(1)} %shard_map.58.x0, bf16[2,4,32,256]{3,2,1,0:T(8,128)(2,1)S(1)} %collective-permute-done.8.x1, bf16[2,4,32,256]{3,2,1,0:T(8,128)(2,1)S(1)} %collective-permute-done.9.x2, bf16[2,4,32,256]{3,2,1,0:T(8,128)(2,1)S(1)} %collective-permute-done.10.x3), custom_call_target="tpu_custom_call" | custom-call | tf_op jit(solution)/shard_map/pallas_call | solution.py:269
Async XLA Ops:
  1.8 12.5 %copy-start = (s32[64]{0:T(128)S(1)}, s32[64]{0:T(128)}, u32[]{:S(2)}) copy-start(s32[64]{0:T(128)} %owner_hbm.1) | copy-start | bytes 772
  1.8 12.5 %copy-start.1 = (s32[5]{0:T(128)S(1)}, s32[5]{0:T(128)}, u32[]{:S(2)}) copy-start(s32[5]{0:T(128)} %port.1) | copy-start | bytes 64
  1.8 9.8 %collective-permute-start.1 = (f32[5,32,256]{2,1,0:T(8,128)S(1)}, f32[5,32,256]{2,1,0:T(8,128)S(1)}, u32[]{:S(2)}, u32[]{:S(2)}) collective-permute-start(f32[5,32,256]{2,1,0:T(8,128)S(1)} %shard_map.56), channel_id=1, source_target_pairs={{0,2},{1,3},{2,0},{3,1},{4,6},{5,7},{6,4},{7,5},{8,10},{9,11},{10,... | collective-permute-start | bytes 491528 | tf_op jit(solution)/shard_map/ppermute | solution.py:28
  8.2 6.0 %collective-permute-start = (f32[5,32,256]{2,1,0:T(8,128)S(1)}, f32[5,32,256]{2,1,0:T(8,128)S(1)}, u32[]{:S(2)}, u32[]{:S(2)}) collective-permute-start(f32[5,32,256]{2,1,0:T(8,128)S(1)} %get-tuple-element.15), channel_id=1, source_target_pairs={{0,1},{1,2},{2,3},{3,0},{4,5},{5,6},{6,7},{7,4},{8,9},{9,10},{10,1... | collective-permute-start | bytes 491528 | tf_op jit(solution)/shard_map/ppermute | solution.py:28
  8.6 5.6 %collective-permute-start.2 = (f32[5,32,256]{2,1,0:T(8,128)S(1)}, f32[5,32,256]{2,1,0:T(8,128)S(1)}, u32[]{:S(2)}, u32[]{:S(2)}) collective-permute-start(f32[5,32,256]{2,1,0:T(8,128)S(1)} %get-tuple-element.16), channel_id=1, source_target_pairs={{0,3},{1,0},{2,1},{3,2},{4,7},{5,4},{6,5},{7,6},{8,11},{9,8},{10,9... | collective-permute-start | bytes 491528 | tf_op jit(solution)/shard_map/ppermute | solution.py:28
  14.9 12.4 %collective-permute-start.3 = (bf16[2,32,256]{2,1,0:T(8,128)(2,1)S(1)}, bf16[2,32,256]{2,1,0:T(8,128)(2,1)S(1)}, u32[]{:S(2)}, u32[]{:S(2)}) collective-permute-start(bf16[2,32,256]{2,1,0:T(8,128)(2,1)S(1)} %get-tuple-element.17), channel_id=1, source_target_pairs={{0,8},{4,12},{8,16},{12,20},{16,24},{20,28},{24,32},{28,36},{32,40... | collective-permute-start | bytes 98312 | tf_op jit(solution)/shard_map/ppermute | solution.py:28
  16.3 11.0 %collective-permute-start.4 = (bf16[2,32,256]{2,1,0:T(8,128)(2,1)S(1)}, bf16[2,32,256]{2,1,0:T(8,128)(2,1)S(1)}, u32[]{:S(2)}, u32[]{:S(2)}) collective-permute-start(bf16[2,32,256]{2,1,0:T(8,128)(2,1)S(1)} %get-tuple-element.18), channel_id=1, source_target_pairs={{0,248},{4,252},{8,0},{12,4},{16,8},{20,12},{24,16},{28,20},{32,24... | collective-permute-start | bytes 98312 | tf_op jit(solution)/shard_map/ppermute | solution.py:28
  23.1 4.8 %collective-permute-start.5 = (bf16[2,32,256]{2,1,0:T(8,128)(2,1)S(1)}, bf16[2,32,256]{2,1,0:T(8,128)(2,1)S(1)}, u32[]{:S(2)}, u32[]{:S(2)}) collective-permute-start(bf16[2,32,256]{2,1,0:T(8,128)(2,1)S(1)} %get-tuple-element.19), channel_id=1, source_target_pairs={{0,244},{4,248},{8,252},{12,0},{16,4},{20,8},{24,12},{28,16},{32,2... | collective-permute-start | bytes 98312 | tf_op jit(solution)/shard_map/ppermute | solution.py:28
  26.8 1.2 %collective-permute-start.6 = (bf16[2,32,256]{2,1,0:T(8,128)(2,1)S(1)}, bf16[2,32,256]{2,1,0:T(8,128)(2,1)S(1)}, u32[]{:S(2)}, u32[]{:S(2)}) collective-permute-start(bf16[2,32,256]{2,1,0:T(8,128)(2,1)S(1)} %get-tuple-element.20), channel_id=1, source_target_pairs={{0,4},{4,8},{8,12},{12,16},{16,20},{20,24},{24,28},{28,32},{32,36}... | collective-permute-start | bytes 98312 | tf_op jit(solution)/shard_map/ppermute | solution.py:28
  26.8 3.6 %collective-permute-start.7 = (bf16[2,32,256]{2,1,0:T(8,128)(2,1)S(1)}, bf16[2,32,256]{2,1,0:T(8,128)(2,1)S(1)}, u32[]{:S(2)}, u32[]{:S(2)}) collective-permute-start(bf16[2,32,256]{2,1,0:T(8,128)(2,1)S(1)} %get-tuple-element.21), channel_id=1, source_target_pairs={{0,252},{4,0},{8,4},{12,8},{16,12},{20,16},{24,20},{28,24},{32,28}... | collective-permute-start | bytes 98312 | tf_op jit(solution)/shard_map/ppermute | solution.py:28
  30.5 5.5 %collective-permute-start.10 = (bf16[2,4,32,256]{3,2,1,0:T(8,128)(2,1)S(1)}, bf16[2,4,32,256]{3,2,1,0:T(8,128)(2,1)S(1)}, u32[]{:S(2)}, u32[]{:S(2)}) collective-permute-start(bf16[2,4,32,256]{3,2,1,0:T(8,128)(2,1)S(1)} %shard_map.58.x0), channel_id=1, source_target_pairs={{0,2},{1,3},{2,0},{3,1},{4,6},{5,7},{6,4},{7,5},{8,10},{9,11},{10,... | collective-permute-start | bytes 393224 | tf_op jit(solution)/shard_map/ppermute | solution.py:28
  31.4 6.9 %collective-permute-start.9 = (bf16[2,4,32,256]{3,2,1,0:T(8,128)(2,1)S(1)}, bf16[2,4,32,256]{3,2,1,0:T(8,128)(2,1)S(1)}, u32[]{:S(2)}, u32[]{:S(2)}) collective-permute-start(bf16[2,4,32,256]{3,2,1,0:T(8,128)(2,1)S(1)} %shard_map.58.x0), channel_id=1, source_target_pairs={{0,1},{1,2},{2,3},{3,0},{4,5},{5,6},{6,7},{7,4},{8,9},{9,10},{10,1... | collective-permute-start | bytes 393224 | tf_op jit(solution)/shard_map/ppermute | solution.py:28
  33.8 5.1 %collective-permute-start.8 = (bf16[2,4,32,256]{3,2,1,0:T(8,128)(2,1)S(1)}, bf16[2,4,32,256]{3,2,1,0:T(8,128)(2,1)S(1)}, u32[]{:S(2)}, u32[]{:S(2)}) collective-permute-start(bf16[2,4,32,256]{3,2,1,0:T(8,128)(2,1)S(1)} %shard_map.58.x0), channel_id=1, source_target_pairs={{0,3},{1,0},{2,1},{3,2},{4,7},{5,4},{6,5},{7,6},{8,11},{9,8},{10,9... | collective-permute-start | bytes 393224 | tf_op jit(solution)/shard_map/ppermute | solution.py:28
